TPU v7x, 128 devices: a whole 4x4x4 slice. The times are simulated.
128 devices in a mesh: visit: 8 (over y_lo, z), patch: 16 (over y_hi, x, core).
Axes of the slice: x: 4, y: 4 (y_hi: 2, y_lo: 2; y = y_hi * 2 + y_lo), z: 4, core: 2. Of those that a mesh axis runs over, the one named last changes fastest.
Arguments:
- pixels: bfloat16 [16, 16, 4, 512, 512], P('patch', 'visit'), may hold values from -6 to 6
- row_mask: int32 [16, 16, 4, 512], P('patch', 'visit'), may hold values 0 or 1
- col_mask: int32 [16, 16, 4, 512], P('patch', 'visit'), may hold values 0 or 1
- route: int32 [16, 16, 4], P('patch', 'visit'), may hold values from 0 to 15, as said below
- tile: int32 [16, 16, 4], P('patch', 'visit'), may hold values from 0 to 3
- wcs_offset: int32 [16, 16, 4, 2], P('patch', 'visit'), may hold values from -8 to 8
- subpixel: bfloat16 [16, 16, 4, 2], P('patch', 'visit'), may hold values from 0 to 1
- plate_scale: bfloat16 [16, 16, 4], P('patch', 'visit'), may hold values from 0.9765625 to 1.015625
- stretch_weight: bfloat16 [16, 16, 4], P('patch', 'visit'), may hold values from 0.25 to 4
- psf_taps: float32 [16, 2, 41], P('visit'), may hold values from 0.05 to 1
Outputs:
- coadd_flux: float32 [1024, 16384], P('visit', 'patch')
- coadd_weight: float32 [1024, 16384], P('visit', 'patch')
- hessian: float32 [16, 10, 10], P('patch')
Inputs may be any that keep to these rules, and one draw needn't show every extreme that they name: `route`: among the stretches of one CCD in one aligned block of 2 visits, at most 2 go to one patch; in every draw one patch receives exactly 2 stretches from every such block.
All inputs are finite; a program needn't handle non-finite values. No bound on the sum of `row_mask` or of `col_mask` on one device may be relied on, other than what follows from the above.
Results may differ from a plain program's by a relative error of at most 0.013.
Values may be sent and summed in bfloat16 or wider, within the bound.
A program may use at most 192 MiB of HBM per device.

v0:
```python
import jax
import jax.numpy as jnp
import numpy as np
from jax import lax
from jax.sharding import PartitionSpec as P

PAIRS = ((0, 0), (1, 0), (0, 1), (2, 0), (1, 1), (0, 2), (3, 0), (2, 1), (1, 2), (0, 3))
precise = lax.Precision.HIGHEST


def extended_2(array, sides, width):
    for axis, dim in sides:
        size, length = (lax.axis_size(axis), array.shape[dim])
        up = [(i, (i + 1) % size) for i in range(size - 1)]
        down = [(j, i) for i, j in up]
        last = lax.slice_in_dim(array, length - width, length, axis=dim)
        leading = lax.slice_in_dim(array, 0, width, axis=dim)
        before = lax.ppermute(last, axis, up)
        after = lax.ppermute(leading, axis, down)
        array = jnp.concatenate([before, array, after], axis=dim)
    return array


def pick_tables():
    row_pick = []
    col_pick = []
    for first in range(10):
        row_line = []
        col_line = []
        for second in range(10):
            row_line.append(PAIRS[first][0] * 4 + PAIRS[second][0])
            col_line.append(PAIRS[first][1] * 4 + PAIRS[second][1])
        row_pick.append(row_line)
        col_pick.append(col_line)
    return (np.array(row_pick), np.array(col_pick))


def lanczos(offset):
    inside = jnp.abs(offset) < 3.0
    return jnp.where(inside, jnp.sinc(offset) * jnp.sinc(offset / 3.0), jnp.zeros_like(offset))


def source_positions(plate_factor, whole_shift, fraction, extent):
    grid_pos = jnp.arange(extent).astype(jnp.float32)
    middle = extent / 2.0
    return (
        plate_factor[:, None] * (grid_pos[None, :] - middle)
        + (middle + (whole_shift + fraction))[:, None]
    )


def legendre(coord):
    square = coord * coord
    return jnp.stack(
        [jnp.ones_like(coord), coord, 1.5 * square - 0.5, (2.5 * square - 1.5) * coord], axis=-2
    )


def resample(cleaned, geometry, mask_pair):
    extent = cleaned.shape[-1]
    plate_factor = geometry[:, 0]
    source_y = source_positions(plate_factor, geometry[:, 3], geometry[:, 1], extent)
    source_x = source_positions(plate_factor, geometry[:, 4], geometry[:, 2], extent)
    grid_pos = jnp.arange(extent).astype(jnp.float32)
    rows_map = (1.0 * lanczos(grid_pos[None, None, :] - source_y[:, :, None])).astype(jnp.bfloat16)
    cols_map = (
        geometry[:, 5][:, None, None] * lanczos(grid_pos[None, None, :] - source_x[:, :, None])
    ).astype(jnp.bfloat16)
    half_warp = jnp.einsum(
        "bim,bmn->bin", rows_map, cleaned, preferred_element_type=jnp.float32
    ).astype(jnp.bfloat16)
    warped = jnp.einsum(
        "bin,bjn->bij", half_warp, cols_map, preferred_element_type=jnp.float32
    ).astype(jnp.bfloat16)
    row_cover = jnp.einsum(
        "bim,bm->bi", rows_map, mask_pair[:, 0], preferred_element_type=jnp.float32
    )
    col_cover = jnp.einsum(
        "bjn,bn->bj", cols_map, mask_pair[:, 1], preferred_element_type=jnp.float32
    )
    covers = jnp.stack([row_cover, col_cover], axis=1).astype(jnp.bfloat16)
    return (warped, covers)


def warp_group(group_data):
    return resample(group_data[0], group_data[1], group_data[2])


def stretch_moments(cleaned, row_block, col_block):
    extent = cleaned.shape[-1]
    grid_pos = jnp.arange(extent).astype(jnp.float32)
    coord_y = (
        row_block.astype(jnp.float32)[:, None] * extent + grid_pos[None, :] + 0.5
    ) / extent - 1.0
    coord_x = (
        col_block.astype(jnp.float32)[:, None] * extent + grid_pos[None, :] + 0.5
    ) / extent - 1.0
    poly_y = legendre(coord_y)
    poly_x = legendre(coord_x)
    outer_y = (
        (poly_y[:, :, None, :] * poly_y[:, None, :, :])
        .reshape(cleaned.shape[0], 16, extent)
        .astype(jnp.bfloat16)
    )
    outer_x = (
        (poly_x[:, :, None, :] * poly_x[:, None, :, :])
        .reshape(cleaned.shape[0], 16, extent)
        .astype(jnp.bfloat16)
    )
    values = cleaned.astype(jnp.float32)
    square = (values * values).astype(jnp.bfloat16)
    partial_rows = jnp.einsum("bpi,bij->bpj", outer_y, square, preferred_element_type=jnp.float32)
    return jnp.einsum("bpj,bqj->bpq", partial_rows, outer_x.astype(jnp.float32), precision=precise)


def toeplitz(tap_rows, count_out, span_cols):
    groups, tap_count = tap_rows.shape
    filler = jnp.zeros((groups, span_cols + 1 - tap_count), tap_rows.dtype)
    period = jnp.concatenate([tap_rows, filler], axis=1)
    repeated = jnp.tile(period, (1, count_out))[:, : count_out * span_cols]
    return repeated.reshape(groups, count_out, span_cols)


def plane_factors(covers, labels):
    extent = covers.shape[-1]
    tile_ids = labels[:, 1].astype(jnp.int32)
    which_row = (jnp.arange(2)[None, :, None] == (tile_ids // 2)[:, None, None]).astype(
        jnp.bfloat16
    )
    which_col = (jnp.arange(2)[None, :, None] == (tile_ids % 2)[:, None, None]).astype(jnp.bfloat16)
    row_factor = (which_row * covers[:, 0][:, None, :]).reshape(-1, 2 * extent)
    col_factor = (which_col * covers[:, 1][:, None, :]).reshape(-1, 2 * extent)
    return (row_factor, col_factor)


def body(
    pixels,
    row_mask,
    col_mask,
    route,
    tile,
    wcs_offset,
    subpixel,
    plate_scale,
    stretch_weight,
    psf_taps,
):
    visits_dev = psf_taps.shape[0]
    extent = pixels.shape[-1]
    pieces = pixels.shape[2]
    stretch_count = visits_dev * pieces
    patch_count = lax.axis_size("patch")
    capacity = max(2, (stretch_count + patch_count - 1) // patch_count)
    slot_count = patch_count * capacity
    patch_side = 2 * extent
    rows_flat = row_mask.reshape(stretch_count, extent).astype(jnp.bfloat16)
    cols_flat = col_mask.reshape(stretch_count, extent).astype(jnp.bfloat16)
    cleaned = pixels.reshape(stretch_count, extent, extent) * (
        rows_flat[:, :, None] * cols_flat[:, None, :]
    )
    mask_pair = jnp.stack([rows_flat, cols_flat], axis=1)
    geometry = jnp.concatenate(
        [
            plate_scale.reshape(stretch_count, 1).astype(jnp.float32),
            subpixel.reshape(stretch_count, 2).astype(jnp.float32),
            wcs_offset.reshape(stretch_count, 2).astype(jnp.float32),
            stretch_weight.reshape(stretch_count, 1).astype(jnp.float32),
        ],
        axis=1,
    )
    stretch_order = jnp.arange(stretch_count)
    labels = jnp.stack(
        [
            (stretch_order // pieces + 1).astype(jnp.float32),
            tile.reshape(stretch_count).astype(jnp.float32),
        ],
        axis=1,
    )
    stretch_gains = stretch_weight.reshape(stretch_count).astype(jnp.float32)
    moments = stretch_moments(cleaned, stretch_order % pieces // 2, stretch_order % 2)
    weighted_moments = jnp.einsum("b,bpq->pq", stretch_gains, moments, precision=precise)
    row_pick, col_pick = pick_tables()
    norm_factor = 1.0 / (visits_dev * lax.axis_size("visit") * pieces * extent * extent)
    hess_local = weighted_moments[row_pick, col_pick] * norm_factor
    hessian = lax.psum(hess_local, "visit")[None]
    destination = route.reshape(stretch_count)
    dest_rank = jnp.sum(
        (destination[:, None] == destination[None, :])
        & (stretch_order[None, :] < stretch_order[:, None]),
        axis=1,
    )
    target_slot = destination * capacity + dest_rank
    placement = jnp.arange(slot_count)[:, None] == target_slot[None, :]
    place_half = placement.astype(jnp.bfloat16)
    extra_cols = jnp.concatenate([geometry, labels], axis=1)
    send_pix = jnp.einsum(
        "sc,cyx->syx", place_half, cleaned, preferred_element_type=jnp.float32
    ).astype(jnp.bfloat16)
    send_vec = jnp.einsum(
        "sc,cvx->svx", place_half, mask_pair, preferred_element_type=jnp.float32
    ).astype(jnp.bfloat16)
    send_extra = jnp.dot(
        place_half, extra_cols.astype(jnp.bfloat16), preferred_element_type=jnp.float32
    ).astype(jnp.bfloat16)
    got_pix, got_vec, got_extra = (
        lax.all_to_all(
            send_pix.reshape(patch_count, capacity, extent, extent),
            "patch",
            split_axis=0,
            concat_axis=0,
            tiled=True,
        ),
        lax.all_to_all(
            send_vec.reshape(patch_count, capacity, 2, extent),
            "patch",
            split_axis=0,
            concat_axis=0,
            tiled=True,
        ),
        lax.all_to_all(
            send_extra.reshape(patch_count, capacity, -1),
            "patch",
            split_axis=0,
            concat_axis=0,
            tiled=True,
        ),
    )
    warped_in, covers_in = lax.map(
        warp_group, (got_pix, got_extra[..., :6].astype(jnp.float32), got_vec)
    )
    warped_slots = warped_in.reshape(slot_count, extent, extent)
    covers_slots = covers_in.reshape(slot_count, 2, extent)
    labels_slots = got_extra[..., -2:].reshape(slot_count, 2)
    visit_tags = labels_slots[:, 0].astype(jnp.int32) - 1
    tile_ids = labels_slots[:, 1].astype(jnp.int32)
    target_tile = visit_tags * 4 + tile_ids
    select = (
        (jnp.arange(visits_dev * 4)[:, None] == target_tile[None, :]) & (visit_tags[None, :] >= 0)
    ).astype(jnp.bfloat16)
    layer_tiles = jnp.einsum(
        "ms,syx->myx", select, warped_slots, preferred_element_type=jnp.float32
    ).astype(jnp.bfloat16)
    layer_image = (
        layer_tiles.reshape(visits_dev, 2, 2, extent, extent)
        .transpose(0, 1, 3, 2, 4)
        .reshape(visits_dev, patch_side, patch_side)
    )
    half_taps = (psf_taps.shape[-1] - 1) // 2
    span_cols = patch_side + 2 * half_taps
    kernels = (psf_taps / jnp.sum(psf_taps, axis=2, keepdims=True)).astype(jnp.bfloat16)
    extended = extended_2(layer_image, (("patch", 2),), half_taps)
    band_x = toeplitz(kernels[:, 0], patch_side, span_cols)
    smooth_x = jnp.einsum(
        "uyr,uar->uya", extended, band_x, preferred_element_type=jnp.float32
    ).astype(jnp.bfloat16)
    padded = jnp.pad(smooth_x, ((0, 0), (half_taps, half_taps), (0, 0)))
    band_y = toeplitz(kernels[:, 1], patch_side, span_cols)
    flux_sum = jnp.einsum("ubr,urx->bx", band_y, padded, preferred_element_type=jnp.float32)
    row_factor, col_factor = plane_factors(covers_slots, labels_slots)
    weight_sum = jnp.dot(row_factor.T, col_factor, preferred_element_type=jnp.float32)
    flux_rows, weight_rows = (
        lax.psum_scatter(flux_sum, "visit", scatter_dimension=0, tiled=True),
        lax.psum_scatter(weight_sum, "visit", scatter_dimension=0, tiled=True),
    )
    return (flux_rows, weight_rows, hessian)


def solution(mesh):
    in_specs = (
        P("patch", "visit", None, None, None),
        P("patch", "visit", None, None),
        P("patch", "visit", None, None),
        P("patch", "visit", None),
        P("patch", "visit", None),
        P("patch", "visit", None, None),
        P("patch", "visit", None, None),
        P("patch", "visit", None),
        P("patch", "visit", None),
        P("visit", None, None),
    )
    out_specs = (P("visit", "patch"), P("visit", "patch"), P("patch", None, None))
    return jax.shard_map(body, mesh=mesh, in_specs=in_specs, out_specs=out_specs, check_vma=False)
```

profile of v0, /device:TPU:29, one launch (start us, length us, event | category | flops | bytes accessed | tf_op | source)
XLA Modules:
  0.0 918.1 jit_solution(8824150413275502546)
XLA Ops:
  44.0 16.8 %copy.85 = bf16[32,512,512]{2,1,0:T(8,128)(2,1)} copy(bf16[32,512,512]{2,0,1:T(8,128)(2,1)} %convolution_convert_fusion.2) | data formatting | bytes 33554432 | tf_op jit(solution)/shard_map/reshape | solution.py:207
  69.7 221.3 %all-to-all-done.1 = bf16[16,2,512,512]{3,2,1,0:T(8,128)(2,1)} async-done(((bf16[16,2,512,512]{3,2,1,0:T(8,128)(2,1)}), bf16[16,2,512,512]{3,2,1,0:T(8,128)(2,1)}, u32[]{:S(2)}, u32[]{:S(2)}) %all-to-all-start.1) | async-done | bytes 16777248 | tf_op jit(solution)/shard_map/all_to_all | solution.py:206
  291.1 382.1 %while.14 = (s32[]{:T(128)}, bf16[16,2,512,512]{3,2,1,0:T(8,128)(2,1)}, bf16[16,2,2,512]{3,1,0,2:T(2,128)(2,1)S(1)}, f32[16,2,6]{2,1,0:T(2,128)S(1)}, bf16[16,2,...) while((s32[]{:T(128)}, bf16[16,2,512,512]{3,2,1,0:T(8,128)(2,1)}, ...), condition=%wide.region_3.5_spmd, body=%wide.region_2.4_spmd.sunk | while | flops 1228943872 | bytes 2178857 | solution.py:228
  291.6 12.7 %fusion.232 = bf16[16,2,512,512]{3,2,1,0:T(8,128)(2,1)} fusion(bf16[16,2,512,512]{3,2,1,0:T(8,128)(2,1)} %get-tuple-element.211, s32[]{:T(128)} %get-tuple-element.210, bf16[16,2,512,512]{3,2,1,0:T(8,128)(2,1)} %get-tuple-element.221, f32[2,512]{1,0:T(2,128)S(1)} %get-tuple-element.196, f32[512]{0:T(512)S(1)} %iota_convert_fusion.3, ...), kind=kOutput, calls=%fused_computation.124.clone.1 | convolution fusion | flops 1150812160 | bytes 2110976 | tf_op jit(solution)/shard_map/while/body/eval_jaxpr/bin,bjn->bij/dot_general | solution.py:72
  315.5 12.7 %fusion.232 = bf16[16,2,512,512]{3,2,1,0:T(8,128)(2,1)} fusion(bf16[16,2,512,512]{3,2,1,0:T(8,128)(2,1)} %get-tuple-element.211, s32[]{:T(128)} %get-tuple-element.210, bf16[16,2,512,512]{3,2,1,0:T(8,128)(2,1)} %get-tuple-element.221, f32[2,512]{1,0:T(2,128)S(1)} %get-tuple-element.196, f32[512]{0:T(512)S(1)} %iota_convert_fusion.3, ...), kind=kOutput, calls=%fused_computation.124.clone.1 | convolution fusion | flops 1150812160 | bytes 2110976 | tf_op jit(solution)/shard_map/while/body/eval_jaxpr/bin,bjn->bij/dot_general | solution.py:72
  339.3 12.7 %fusion.232 = bf16[16,2,512,512]{3,2,1,0:T(8,128)(2,1)} fusion(bf16[16,2,512,512]{3,2,1,0:T(8,128)(2,1)} %get-tuple-element.211, s32[]{:T(128)} %get-tuple-element.210, bf16[16,2,512,512]{3,2,1,0:T(8,128)(2,1)} %get-tuple-element.221, f32[2,512]{1,0:T(2,128)S(1)} %get-tuple-element.196, f32[512]{0:T(512)S(1)} %iota_convert_fusion.3, ...), kind=kOutput, calls=%fused_computation.124.clone.1 | convolution fusion | flops 1150812160 | bytes 2110976 | tf_op jit(solution)/shard_map/while/body/eval_jaxpr/bin,bjn->bij/dot_general | solution.py:72
  363.2 12.7 %fusion.232 = bf16[16,2,512,512]{3,2,1,0:T(8,128)(2,1)} fusion(bf16[16,2,512,512]{3,2,1,0:T(8,128)(2,1)} %get-tuple-element.211, s32[]{:T(128)} %get-tuple-element.210, bf16[16,2,512,512]{3,2,1,0:T(8,128)(2,1)} %get-tuple-element.221, f32[2,512]{1,0:T(2,128)S(1)} %get-tuple-element.196, f32[512]{0:T(512)S(1)} %iota_convert_fusion.3, ...), kind=kOutput, calls=%fused_computation.124.clone.1 | convolution fusion | flops 1150812160 | bytes 2110976 | tf_op jit(solution)/shard_map/while/body/eval_jaxpr/bin,bjn->bij/dot_general | solution.py:72
  387.0 12.7 %fusion.232 = bf16[16,2,512,512]{3,2,1,0:T(8,128)(2,1)} fusion(bf16[16,2,512,512]{3,2,1,0:T(8,128)(2,1)} %get-tuple-element.211, s32[]{:T(128)} %get-tuple-element.210, bf16[16,2,512,512]{3,2,1,0:T(8,128)(2,1)} %get-tuple-element.221, f32[2,512]{1,0:T(2,128)S(1)} %get-tuple-element.196, f32[512]{0:T(512)S(1)} %iota_convert_fusion.3, ...), kind=kOutput, calls=%fused_computation.124.clone.1 | convolution fusion | flops 1150812160 | bytes 2110976 | tf_op jit(solution)/shard_map/while/body/eval_jaxpr/bin,bjn->bij/dot_general | solution.py:72
  410.9 12.7 %fusion.232 = bf16[16,2,512,512]{3,2,1,0:T(8,128)(2,1)} fusion(bf16[16,2,512,512]{3,2,1,0:T(8,128)(2,1)} %get-tuple-element.211, s32[]{:T(128)} %get-tuple-element.210, bf16[16,2,512,512]{3,2,1,0:T(8,128)(2,1)} %get-tuple-element.221, f32[2,512]{1,0:T(2,128)S(1)} %get-tuple-element.196, f32[512]{0:T(512)S(1)} %iota_convert_fusion.3, ...), kind=kOutput, calls=%fused_computation.124.clone.1 | convolution fusion | flops 1150812160 | bytes 2110976 | tf_op jit(solution)/shard_map/while/body/eval_jaxpr/bin,bjn->bij/dot_general | solution.py:72
  434.8 12.7 %fusion.232 = bf16[16,2,512,512]{3,2,1,0:T(8,128)(2,1)} fusion(bf16[16,2,512,512]{3,2,1,0:T(8,128)(2,1)} %get-tuple-element.211, s32[]{:T(128)} %get-tuple-element.210, bf16[16,2,512,512]{3,2,1,0:T(8,128)(2,1)} %get-tuple-element.221, f32[2,512]{1,0:T(2,128)S(1)} %get-tuple-element.196, f32[512]{0:T(512)S(1)} %iota_convert_fusion.3, ...), kind=kOutput, calls=%fused_computation.124.clone.1 | convolution fusion | flops 1150812160 | bytes 2110976 | tf_op jit(solution)/shard_map/while/body/eval_jaxpr/bin,bjn->bij/dot_general | solution.py:72
  458.7 12.7 %fusion.232 = bf16[16,2,512,512]{3,2,1,0:T(8,128)(2,1)} fusion(bf16[16,2,512,512]{3,2,1,0:T(8,128)(2,1)} %get-tuple-element.211, s32[]{:T(128)} %get-tuple-element.210, bf16[16,2,512,512]{3,2,1,0:T(8,128)(2,1)} %get-tuple-element.221, f32[2,512]{1,0:T(2,128)S(1)} %get-tuple-element.196, f32[512]{0:T(512)S(1)} %iota_convert_fusion.3, ...), kind=kOutput, calls=%fused_computation.124.clone.1 | convolution fusion | flops 1150812160 | bytes 2110976 | tf_op jit(solution)/shard_map/while/body/eval_jaxpr/bin,bjn->bij/dot_general | solution.py:72
  482.6 12.7 %fusion.232 = bf16[16,2,512,512]{3,2,1,0:T(8,128)(2,1)} fusion(bf16[16,2,512,512]{3,2,1,0:T(8,128)(2,1)} %get-tuple-element.211, s32[]{:T(128)} %get-tuple-element.210, bf16[16,2,512,512]{3,2,1,0:T(8,128)(2,1)} %get-tuple-element.221, f32[2,512]{1,0:T(2,128)S(1)} %get-tuple-element.196, f32[512]{0:T(512)S(1)} %iota_convert_fusion.3, ...), kind=kOutput, calls=%fused_computation.124.clone.1 | convolution fusion | flops 1150812160 | bytes 2110976 | tf_op jit(solution)/shard_map/while/body/eval_jaxpr/bin,bjn->bij/dot_general | solution.py:72
  506.4 12.7 %fusion.232 = bf16[16,2,512,512]{3,2,1,0:T(8,128)(2,1)} fusion(bf16[16,2,512,512]{3,2,1,0:T(8,128)(2,1)} %get-tuple-element.211, s32[]{:T(128)} %get-tuple-element.210, bf16[16,2,512,512]{3,2,1,0:T(8,128)(2,1)} %get-tuple-element.221, f32[2,512]{1,0:T(2,128)S(1)} %get-tuple-element.196, f32[512]{0:T(512)S(1)} %iota_convert_fusion.3, ...), kind=kOutput, calls=%fused_computation.124.clone.1 | convolution fusion | flops 1150812160 | bytes 2110976 | tf_op jit(solution)/shard_map/while/body/eval_jaxpr/bin,bjn->bij/dot_general | solution.py:72
  530.3 12.7 %fusion.232 = bf16[16,2,512,512]{3,2,1,0:T(8,128)(2,1)} fusion(bf16[16,2,512,512]{3,2,1,0:T(8,128)(2,1)} %get-tuple-element.211, s32[]{:T(128)} %get-tuple-element.210, bf16[16,2,512,512]{3,2,1,0:T(8,128)(2,1)} %get-tuple-element.221, f32[2,512]{1,0:T(2,128)S(1)} %get-tuple-element.196, f32[512]{0:T(512)S(1)} %iota_convert_fusion.3, ...), kind=kOutput, calls=%fused_computation.124.clone.1 | convolution fusion | flops 1150812160 | bytes 2110976 | tf_op jit(solution)/shard_map/while/body/eval_jaxpr/bin,bjn->bij/dot_general | solution.py:72
  554.2 12.7 %fusion.232 = bf16[16,2,512,512]{3,2,1,0:T(8,128)(2,1)} fusion(bf16[16,2,512,512]{3,2,1,0:T(8,128)(2,1)} %get-tuple-element.211, s32[]{:T(128)} %get-tuple-element.210, bf16[16,2,512,512]{3,2,1,0:T(8,128)(2,1)} %get-tuple-element.221, f32[2,512]{1,0:T(2,128)S(1)} %get-tuple-element.196, f32[512]{0:T(512)S(1)} %iota_convert_fusion.3, ...), kind=kOutput, calls=%fused_computation.124.clone.1 | convolution fusion | flops 1150812160 | bytes 2110976 | tf_op jit(solution)/shard_map/while/body/eval_jaxpr/bin,bjn->bij/dot_general | solution.py:72
  578.1 12.7 %fusion.232 = bf16[16,2,512,512]{3,2,1,0:T(8,128)(2,1)} fusion(bf16[16,2,512,512]{3,2,1,0:T(8,128)(2,1)} %get-tuple-element.211, s32[]{:T(128)} %get-tuple-element.210, bf16[16,2,512,512]{3,2,1,0:T(8,128)(2,1)} %get-tuple-element.221, f32[2,512]{1,0:T(2,128)S(1)} %get-tuple-element.196, f32[512]{0:T(512)S(1)} %iota_convert_fusion.3, ...), kind=kOutput, calls=%fused_computation.124.clone.1 | convolution fusion | flops 1150812160 | bytes 2110976 | tf_op jit(solution)/shard_map/while/body/eval_jaxpr/bin,bjn->bij/dot_general | solution.py:72
  601.9 12.7 %fusion.232 = bf16[16,2,512,512]{3,2,1,0:T(8,128)(2,1)} fusion(bf16[16,2,512,512]{3,2,1,0:T(8,128)(2,1)} %get-tuple-element.211, s32[]{:T(128)} %get-tuple-element.210, bf16[16,2,512,512]{3,2,1,0:T(8,128)(2,1)} %get-tuple-element.221, f32[2,512]{1,0:T(2,128)S(1)} %get-tuple-element.196, f32[512]{0:T(512)S(1)} %iota_convert_fusion.3, ...), kind=kOutput, calls=%fused_computation.124.clone.1 | convolution fusion | flops 1150812160 | bytes 2110976 | tf_op jit(solution)/shard_map/while/body/eval_jaxpr/bin,bjn->bij/dot_general | solution.py:72
  625.8 12.7 %fusion.232 = bf16[16,2,512,512]{3,2,1,0:T(8,128)(2,1)} fusion(bf16[16,2,512,512]{3,2,1,0:T(8,128)(2,1)} %get-tuple-element.211, s32[]{:T(128)} %get-tuple-element.210, bf16[16,2,512,512]{3,2,1,0:T(8,128)(2,1)} %get-tuple-element.221, f32[2,512]{1,0:T(2,128)S(1)} %get-tuple-element.196, f32[512]{0:T(512)S(1)} %iota_convert_fusion.3, ...), kind=kOutput, calls=%fused_computation.124.clone.1 | convolution fusion | flops 1150812160 | bytes 2110976 | tf_op jit(solution)/shard_map/while/body/eval_jaxpr/bin,bjn->bij/dot_general | solution.py:72
  649.7 12.7 %fusion.232 = bf16[16,2,512,512]{3,2,1,0:T(8,128)(2,1)} fusion(bf16[16,2,512,512]{3,2,1,0:T(8,128)(2,1)} %get-tuple-element.211, s32[]{:T(128)} %get-tuple-element.210, bf16[16,2,512,512]{3,2,1,0:T(8,128)(2,1)} %get-tuple-element.221, f32[2,512]{1,0:T(2,128)S(1)} %get-tuple-element.196, f32[512]{0:T(512)S(1)} %iota_convert_fusion.3, ...), kind=kOutput, calls=%fused_computation.124.clone.1 | convolution fusion | flops 1150812160 | bytes 2110976 | tf_op jit(solution)/shard_map/while/body/eval_jaxpr/bin,bjn->bij/dot_general | solution.py:72
  677.2 16.9 %fusion.168 = bf16[8,512,512]{2,0,1:T(8,128)(2,1)} fusion(bf16[32,512,512]{2,1,0:T(8,128)(2,1)} %bitcast.123, s32[32]{0:T(128)S(1)} %copy-done.4, pred[32]{0:T(512)(128)(4,1)S(1)} %compare_bitcast_fusion), kind=kOutput, calls=%fused_computation.200 | convolution fusion | flops 136315392 | bytes 20971680 | tf_op jit(solution)/shard_map/ms,syx->myx/dot_general | solution.py:240
  772.7 11.3 %reshape.850 = bf16[2181120]{0:T(1024)(128)(2,1)} reshape(bf16[2,1024,1065]{2,1,0:T(8,128)(2,1)} %tile.8) | data formatting | bytes 8724480
  812.6 22.8 %concatenate.29 = bf16[2,1024,1064]{1,2,0:T(8,128)(2,1)} concatenate(bf16[2,1024,20]{1,2,0:T(8,128)(2,1)S(1)} %collective-permute-done, bf16[2,1024,1024]{1,2,0:T(8,128)(2,1)} %copy.65, bf16[2,1024,20]{1,2,0:T(8,128)(2,1)S(1)} %collective-permute-done.1), dimensions={2} | concatenate | bytes 8716288 | tf_op jit(solution)/shard_map/concatenate | solution.py:20
  858.5 17.7 %psum.7 = f32[1,10,10]{2,1,0:T(8,128)S(1)} all-reduce(f32[1,10,10]{2,1,0:T(8,128)S(1)} %broadcast_in_dim.23), channel_id=1, replica_groups=mesh['visit'=8,'patch'=16] {'visit'}, use_global_device_ids=true, to_apply=%region_6.8 | all-reduce | flops 100 | bytes 800 | tf_op jit(solution)/shard_map/psum | solution.py:185
  876.8 34.2 %reduce-scatter.3.cloned.1.call-done = f32[128,1024]{1,0:T(8,128)} async-done(((f32[1024,1024]{1,0:T(8,128)}), f32[128,1024]{1,0:T(8,128)}) %reduce-scatter.3.cloned.1.call-update) | async-done | bytes 524304 | tf_op jit(solution)/shard_map/reduce_scatter | solution.py:262
  (298 shorter events, 358.5 us)
Async XLA Ops:
  12.8 14.0 %all-to-all-start = ((bf16[16,2,8]{2,1,0:T(2,128)(2,1)}), bf16[16,2,8]{2,1,0:T(2,128)(2,1)S(1)}, u32[]{:S(2)}, u32[]{:S(2)}) async-start(bf16[16,2,8]{2,1,0:T(2,128)(2,1)} %bitcast.12), calls=%async_computation | async-start | bytes 16384 | tf_op jit(solution)/shard_map/all_to_all | solution.py:220
  26.9 33.9 %all-to-all-start.2 = ((bf16[16,2,2,512]{3,1,2,0:T(2,128)(2,1)}), bf16[16,2,2,512]{3,1,2,0:T(2,128)(2,1)S(1)}, u32[]{:S(2)}, u32[]{:S(2)}) async-start(bf16[16,2,2,512]{3,1,2,0:T(2,128)(2,1)} %copy.62), calls=%async_computation.2 | async-start | bytes 131072 | tf_op jit(solution)/shard_map/all_to_all | solution.py:213
  60.8 230.3 %all-to-all-start.1 = ((bf16[16,2,512,512]{3,2,1,0:T(8,128)(2,1)}), bf16[16,2,512,512]{3,2,1,0:T(8,128)(2,1)}, u32[]{:S(2)}, u32[]{:S(2)}) async-start(bf16[16,2,512,512]{3,2,1,0:T(8,128)(2,1)} %bitcast.122), calls=%async_computation.1 | async-start | bytes 33554432 | tf_op jit(solution)/shard_map/all_to_all | solution.py:206
  68.0 808.8 %reduce-scatter.5.cloned.1.call-start = ((), (), s32[]{:S(2)}) async-start(), calls=%async_computation.6 | async-start | bytes 4718592 | tf_op jit(solution)/shard_map/reduce_scatter | solution.py:263
  68.3 222.7 %copy-start.5 = (bf16[32,1]{0,1:T(2,128)(2,1)}, bf16[32,1]{0,1:T(2,128)(2,1)S(1)}, u32[]{:S(2)}) copy-start(bf16[32,1]{0,1:T(2,128)(2,1)S(1)} %copy.90) | copy-start | bytes 196
  291.1 382.2 %copy-start.2 = (bf16[32,2]{1,0:T(8,128)(2,1)S(1)}, bf16[32,2]{1,0:T(8,128)(2,1)}, u32[]{:S(2)}) copy-start(bf16[32,2]{1,0:T(8,128)(2,1)} %get-tuple-element.142) | copy-start | bytes 388
  291.1 382.4 %copy-start.1 = (bf16[32,2]{1,0:T(8,128)(2,1)S(1)}, bf16[32,2]{1,0:T(8,128)(2,1)}, u32[]{:S(2)}) copy-start(bf16[32,2]{1,0:T(8,128)(2,1)} %get-tuple-element.143) | copy-start | bytes 388
  676.3 0.7 copy-start.3
  676.3 0.9 copy-start.6
  676.3 0.9 copy-start.4
  676.3 234.6 %reduce-scatter.3.cloned.1.call-start = ((), (), s32[]{:S(2)}) async-start(), calls=%async_computation.5 | async-start | bytes 4718592 | tf_op jit(solution)/shard_map/reduce_scatter | solution.py:262
  723.5 89.1 %collective-permute-start = (bf16[2,1024,20]{1,2,0:T(8,128)(2,1)S(1)}, bf16[2,1024,20]{1,2,0:T(8,128)(2,1)S(1)}, u32[]{:S(2)}, u32[]{:S(2)}) collective-permute-start(bf16[2,1024,20]{1,2,0:T(8,128)(2,1)S(1)} %get-tuple-element.119), channel_id=1, source_target_pairs={{0,1},{1,2},{2,3},{3,4},{4,5},{5,6},{6,7},{7,8},{8,9},{9,10},{10,1... | collective-permute-start | bytes 245768 | tf_op jit(solution)/shard_map/ppermute | solution.py:18
  725.4 87.2 %collective-permute-start.1 = (bf16[2,1024,20]{1,2,0:T(8,128)(2,1)S(1)}, bf16[2,1024,20]{1,2,0:T(8,128)(2,1)S(1)}, u32[]{:S(2)}, u32[]{:S(2)}) collective-permute-start(bf16[2,1024,20]{1,2,0:T(8,128)(2,1)S(1)} %get-tuple-element.118), channel_id=1, source_target_pairs={{1,0},{2,1},{3,2},{4,3},{5,4},{6,5},{7,6},{8,7},{9,8},{10,9},{11,1... | collective-permute-start | bytes 245768 | tf_op jit(solution)/shard_map/ppermute | solution.py:19
  812.6 32.7 %slice-start = ((s8[4718592]{0:T(1024)(128)(4,1)}), s8[524288]{0:T(1024)(128)(4,1)S(1)}, s32[]{:S(2)}) async-start(s8[4718592]{0:T(1024)(128)(4,1)} %bitcast.125), calls=%async_computation.7 | async-start | bytes 1048576
  835.4 9.9 %slice-start.1 = ((s8[4718592]{0:T(1024)(128)(4,1)}), s8[4194304]{0:T(1024)(128)(4,1)S(1)}, s32[]{:S(2)}) async-start(s8[4718592]{0:T(1024)(128)(4,1)} %bitcast.125), calls=%async_computation.8 | async-start | bytes 8388608
  852.0 0.7 copy-start.7
  853.2 3.5 copy-start
Sparse Core Ops, SparseCore 0:
  676.4 55.4 reduce-scatter.4
  852.1 58.7 reduce-scatter.2
where the time goes:
time: 927 us; the launch traced here: 918 us
  matrix products  426 us (46%)
  waiting for transfers between devices  256 us (28%)
  local copies, waits for them, and re-layouts  163 us (18%)
  starting transfers between devices  26.8 us (3%)
  blocking collectives  17.7 us (2%)
  between operations  14.6 us (2%)
  other arithmetic  14.1 us (2%)
    all_to_all x1, waiting for transfers between devices, body(): lax.all_to_all(send_pix.reshape(patch_count, capacity, extent, extent), '...  221 us
    dot_general x16, matrix products, resample(): jnp.einsum('bin,bjn->bij', half_warp, cols_map, preferred_element_type=jn...  203 us
    dot_general x16, matrix products, resample(): jnp.einsum('bjn,bn->bj', cols_map, mask_pair[:, 1], preferred_element_typ...  87.7 us
    dot_general x16, matrix products, resample(): jnp.einsum('bim,bm->bi', rows_map, mask_pair[:, 0], preferred_element_typ...  85 us
    unnamed x31, local copies, waits for them, and re-layouts  39.8 us
    reduce_scatter x1, waiting for transfers between devices, body(): lax.psum_scatter(flux_sum, 'visit', scatter_dimension=0, tiled=True)  34.2 us
    concatenate x1, local copies, waits for them, and re-layouts, extended_2(): array = jnp.concatenate([before, array, after], axis=dim)  22.8 us
    reshape x2, local copies, waits for them, and re-layouts, toeplitz(): return repeated.reshape(groups, count_out, span_cols)  20.9 us
  transfers between devices with their start and end apart: 7, of which 2 were waited for; matrix products, arithmetic and copies ran while one was open for 23% of the time, Pallas kernels for 0%

commit v1 on v0

v1 whole, which is shorter than its diff:
```python
import jax
import jax.numpy as jnp
import numpy as np
from jax import lax
from jax.experimental import pallas as pl
from jax.experimental.pallas import tpu as pltpu
from jax.sharding import PartitionSpec as P

PAIRS = ((0, 0), (1, 0), (0, 1), (2, 0), (1, 1), (0, 2), (3, 0), (2, 1), (1, 2), (0, 3))
MESH = pl.DeviceIdType.MESH
precise = lax.Precision.HIGHEST
f32 = jnp.float32
bf16 = jnp.bfloat16
S = 512
TAPS = 41
NP = 16
NV = 8
NS = 8
ROWS = S // NP
HOT = NP - 1


def lanczos(offset):
    inside = jnp.abs(offset) < 3.0
    return jnp.where(inside, jnp.sinc(offset) * jnp.sinc(offset / 3.0), jnp.zeros_like(offset))


def legendre(coord):
    square = coord * coord
    return jnp.stack(
        [jnp.ones_like(coord), coord, 1.5 * square - 0.5, (2.5 * square - 1.5) * coord], axis=-2
    )


def outer_tables():
    grid_pos = jnp.arange(S).astype(f32)
    block = jnp.arange(2).astype(f32)
    coord = (block[:, None] * S + grid_pos[None, :] + 0.5) / S - 1.0
    poly = legendre(coord)
    return (poly[:, :, None, :] * poly[:, None, :, :]).reshape(2, 16, S).astype(bf16)


def dot(a, b, precision=None):
    return jnp.dot(a, b, preferred_element_type=f32, precision=precision)


def dot_nt(a, b, precision=None):
    return lax.dot_general(
        a, b, (((1,), (1,)), ((), ())), preferred_element_type=f32, precision=precision
    )


def dot_tn(a, b):
    return lax.dot_general(a, b, (((0,), (0,)), ((), ())), preferred_element_type=f32)


def band(position, base, weight_of):
    offset = position - base
    value = jnp.zeros(offset.shape, f32)
    for k in range(6):
        value = jnp.where(offset == float(k), weight_of(k), value)
    return value


def tap_matrix(kern, line, shape, shift):
    at = (
        lax.broadcasted_iota(jnp.int32, shape, 0)
        - lax.broadcasted_iota(jnp.int32, shape, 1)
    )
    at = shift(at)

    def one(m, value):
        return jnp.where(at == m, kern[line, m], value)

    return lax.fori_loop(0, TAPS, one, jnp.zeros(shape, f32))


def warp_kernel(
    kern, trow, gain, pix, wts, oy, ox, pp, extra,
    recv, rfr, rsmall, hess, vmat,
    sbuf, fbuf, wpad, ybuf, half, umat, cov, rmom, small, msend, mrecv,
    send_sem, recv_sem, fsend, frecv, ssend, srecv, msend_sem, mrecv_sem,
):
    me_v = lax.axis_index("visit")
    me = lax.axis_index("patch")
    wpad[0:192, :] = jnp.zeros((192, S), bf16)
    wpad[704:896, :] = jnp.zeros((192, S), bf16)
    rmom[...] = jnp.zeros_like(rmom)
    for v in range(2):
        umat[v] = tap_matrix(kern, 2 * v + 1, (128, 256), lambda at: -at - 44).astype(bf16)

    def stretch(s, carry):
        v = s // 4
        piece = s % 4
        is_low = trow[s] == 0
        wt = wts[s]
        columns = jnp.transpose(wt[0:8])
        row_mask = wt[7:8]
        col_mask = wt[15:16]
        ones = jnp.ones((8, 384), bf16)
        for a in range(2):
            at = lax.broadcasted_iota(jnp.int32, (256, 384), 1).astype(f32) + float(128 * a)
            cols = columns[256 * a : 256 * a + 256]
            weights = band(at, cols[:, 6:7], lambda k: cols[:, k : k + 1])
            rows_map = (weights * row_mask[:, 128 * a : 128 * a + 384]).astype(bf16)
            part = dot(rows_map, pix[s, 128 * a : 128 * a + 384, :])
            half[256 * a : 256 * a + 256, :] = (part * col_mask).astype(bf16)
            cover = dot_nt(ones, rows_map)
            cov[pl.ds(s, 1), 256 * a : 256 * a + 256] = cover[0:1]
        for b in range(2):
            at = lax.broadcasted_iota(jnp.int32, (384, 256), 0).astype(f32) + float(128 * b)
            lanes = wt[:, 256 * b : 256 * b + 256]
            cols_map = band(at, lanes[14:15], lambda k: lanes[8 + k : 9 + k]).astype(bf16)
            part = dot(half[:, 128 * b : 128 * b + 384], cols_map)
            wpad[192:704, 256 * b : 256 * b + 256] = part.astype(bf16)
            mask = jnp.broadcast_to(col_mask[:, 128 * b : 128 * b + 384], (8, 384)).astype(bf16)
            cover = dot(mask, cols_map)
            cov[pl.ds(s, 1), S + 256 * b : S + 256 * b + 256] = cover[0:1]
        for a in range(4):
            ybuf[128 * a : 128 * a + 128, :] = dot(
                umat[v], wpad[128 + 128 * a : 384 + 128 * a, :]
            )
        above = dot(umat[v, 96:128, :], wpad[0:256, :])
        below = dot(umat[v, 0:32, :], wpad[640:896, :])
        fbuf[s] = jnp.where(is_low, below, above).astype(bf16)
        for q in range(NP):
            low = ybuf[ROWS * q : ROWS * (q + 1), :]
            high = ybuf[ROWS * (NP - 1 - q) : ROWS * (NP - q), :]
            sbuf[s, ROWS * q : ROWS * (q + 1), :] = jnp.where(is_low, low, high).astype(bf16)

        def send(j, carry):
            k = lax.rem(me + j, NP)
            pltpu.make_async_remote_copy(
                src_ref=sbuf.at[s, pl.ds(pl.multiple_of(k * ROWS, ROWS), ROWS)],
                dst_ref=recv.at[me, s],
                send_sem=send_sem.at[s],
                recv_sem=recv_sem.at[s],
                device_id={"patch": k},
                device_id_type=MESH,
            ).start()
            return carry

        lax.fori_loop(1, NP, send, 0)
        pltpu.make_async_copy(
            sbuf.at[s, pl.ds(pl.multiple_of(me * ROWS, ROWS), ROWS)], recv.at[me, s], recv_sem.at[s]
        ).start()

        @pl.when(me != HOT)
        def _():
            pltpu.make_async_remote_copy(
                src_ref=fbuf.at[s],
                dst_ref=rfr.at[me, s],
                send_sem=fsend.at[s],
                recv_sem=frecv.at[s],
                device_id={"patch": HOT},
                device_id_type=MESH,
            ).start()

        @pl.when(me == HOT)
        def _():
            pltpu.make_async_copy(fbuf.at[s], rfr.at[me, s], frecv.at[s]).start()

        values = pix[s].astype(f32)
        square = (values * values).astype(bf16)
        lhs = oy[piece // 2] * row_mask.astype(bf16)
        rmom[piece % 2] += dot(lhs, square) * (col_mask * gain[s])
        return carry

    lax.fori_loop(0, NS, stretch, 0)

    covers = cov[...].astype(bf16)
    slots = dot(pp[0], covers[:, 0:256])
    for b in range(1, 4):
        slots += dot(pp[b], covers[:, 256 * b : 256 * b + 256])
    small[:, 0:256] = slots
    small[:, 256:384] = extra[...]
    msend[...] = dot_nt(rmom[0], ox[0], precise) + dot_nt(rmom[1], ox[1], precise)

    def send_small(j, carry):
        k = lax.rem(me + j, NP)
        pltpu.make_async_remote_copy(
            src_ref=small.at[pl.ds(pl.multiple_of(k * 8, 8), 8)],
            dst_ref=rsmall.at[me],
            send_sem=ssend,
            recv_sem=srecv,
            device_id={"patch": k},
            device_id_type=MESH,
        ).start()
        return carry

    lax.fori_loop(1, NP, send_small, 0)
    pltpu.make_async_copy(
        small.at[pl.ds(pl.multiple_of(me * 8, 8), 8)], rsmall.at[me], srecv
    ).start()

    def send_moment(j, carry):
        pltpu.make_async_remote_copy(
            src_ref=msend,
            dst_ref=mrecv.at[me_v],
            send_sem=msend_sem,
            recv_sem=mrecv_sem,
            device_id={"visit": lax.rem(me_v + j, NV)},
            device_id_type=MESH,
        ).start()
        return carry

    lax.fori_loop(1, NV, send_moment, 0)
    pltpu.make_async_copy(msend, mrecv.at[me_v], mrecv_sem).start()

    for v in range(2):
        for c in range(4):
            vmat[v, 128 * c : 128 * c + 128, :] = tap_matrix(
                kern, 2 * v, (128, 256), lambda at: at + (128 * c - 108)
            ).astype(bf16)

    pltpu.make_async_copy(mrecv, mrecv, mrecv_sem).wait()
    total = mrecv[0]
    for v in range(1, NV):
        total += mrecv[v]
    hess[...] = total
    pltpu.make_async_copy(mrecv.at[1:NV], mrecv.at[1:NV], msend_sem).wait()
    pltpu.make_async_copy(rsmall, rsmall, srecv).wait()
    pltpu.make_async_copy(rsmall.at[1:NP], rsmall.at[1:NP], ssend).wait()

    def finish(s, carry):
        everyone = recv.at[:, s]
        others = recv.at[1:NP, s]
        pltpu.make_async_copy(everyone, everyone, recv_sem.at[s]).wait()
        pltpu.make_async_copy(others, others, send_sem.at[s]).wait()

        @pl.when(me != HOT)
        def _():
            pltpu.make_async_copy(fbuf.at[s], fbuf.at[s], fsend.at[s]).wait()

        @pl.when(me == HOT)
        def _():
            pltpu.make_async_copy(rfr.at[:, s], rfr.at[:, s], frecv.at[s]).wait()

        return carry

    lax.fori_loop(0, NS, finish, 0)


def layer_kernel(codes, recv, rfr, vmat, out, acc, fvm, sem):
    me = lax.axis_index("patch")
    zero = jnp.zeros((ROWS, 256), f32)

    def clear(b, carry):
        for v in range(2):
            for t in range(2):
                acc[v, t, b] = zero
        return carry

    lax.fori_loop(0, 66, clear, 0)

    def place(at, s, value, flip):
        code = codes[at]
        tile = code % 4
        g = 2 * (code // 4) + tile % 2
        t = tile // 2
        if flip:
            t = 1 - t
        data = value.astype(f32)
        acc[s // 4, t, 2 * g + 1] += data[:, 0:256]
        acc[s // 4, t, 2 * g + 2] += data[:, 256:512]

    def add(at, carry):
        s = at % NS
        place(at, s, recv[at // NS, s], False)
        return carry

    lax.fori_loop(0, NP * NS, add, 0)

    @pl.when(me == HOT)
    def _():
        copy = pltpu.make_async_copy(rfr, fvm, sem)
        copy.start()
        copy.wait()

        def add_fringe(at, carry):
            s = at % NS
            place(at, s, fvm[at // NS, s], True)
            return carry

        lax.fori_loop(0, NP * NS, add_fringe, 0)

    for t in range(2):
        for c in range(4):
            total = None
            for v in range(2):
                block = acc[v, t, 16 * c : 16 * c + 18].reshape(18 * ROWS, 256).astype(bf16)
                left = block[0 : 16 * ROWS, 128:256]
                middle = block[ROWS : 17 * ROWS]
                right = block[2 * ROWS : 18 * ROWS, 0:128]
                part = dot(middle, vmat[v, 128:384])
                part += dot(left, vmat[v, 0:128])
                part += dot(right, vmat[v, 384:512])
                total = part if total is None else total + part
            out[t, 16 * c : 16 * c + 16] = total.astype(bf16).reshape(16, ROWS, 256)


def owner_kernel(slab, wmsg, flux, weight, frecv, wrecv, send_sem, recv_sem, wsend_sem, wrecv_sem):
    me_v = lax.axis_index("visit")
    me = lax.axis_index("patch")
    for t in range(2):
        block = me if t == 0 else NP - 1 - me
        r = 4 * t + block // 4
        slot = lax.rem(block, 4)

        def send(j, carry):
            p = lax.rem(me + j, NP)
            src = slab.at[t, pl.ds(4 * p, 4)]
            dst = frecv.at[me_v, slot]
            mine = (r == me_v) & (p == me)

            @pl.when(jnp.logical_not(mine))
            def _():
                pltpu.make_async_remote_copy(
                    src_ref=src,
                    dst_ref=dst,
                    send_sem=send_sem,
                    recv_sem=recv_sem,
                    device_id={"visit": r, "patch": p},
                    device_id_type=MESH,
                ).start()

            @pl.when(mine)
            def _():
                pltpu.make_async_copy(src, dst, recv_sem).start()

            return carry

        lax.fori_loop(0, NP, send, 0)

    def send_weight(j, carry):
        r = lax.rem(me_v + j, NV)
        pltpu.make_async_remote_copy(
            src_ref=wmsg.at[r],
            dst_ref=wrecv.at[me_v],
            send_sem=wsend_sem,
            recv_sem=wrecv_sem,
            device_id={"visit": r},
            device_id_type=MESH,
        ).start()
        return carry

    lax.fori_loop(1, NV, send_weight, 0)
    pltpu.make_async_copy(wmsg.at[me_v], wrecv.at[me_v], wrecv_sem).start()
    pltpu.make_async_copy(wrecv, wrecv, wrecv_sem).wait()
    cols = wrecv[:, :, 0:512].reshape(NV * 2 * NP, 512)
    left = wrecv[:, :, 512:640].reshape(NV * 2 * NP, 128)
    right = wrecv[:, :, 640:768].reshape(NV * 2 * NP, 128)
    weight[:, 0:512] = dot_tn(left, cols)
    weight[:, 512:1024] = dot_tn(right, cols)
    pltpu.make_async_copy(frecv, frecv, recv_sem).wait()
    for slot in range(4):
        for q in range(4):
            total = frecv[0, slot, q].astype(f32)
            for v in range(1, NV):
                total += frecv[v, slot, q].astype(f32)
            flux[32 * slot : 32 * slot + 32, 256 * q : 256 * q + 256] = total
    pltpu.make_async_copy(wrecv.at[1:NV], wrecv.at[1:NV], wsend_sem).wait()
    is_mine = (me_v == me // 4) | (me_v == 4 + (NP - 1 - me) // 4)

    @pl.when(is_mine)
    def _():
        pltpu.make_async_copy(slab.at[0, 0:60], slab.at[0, 0:60], send_sem).wait()
        pltpu.make_async_copy(slab.at[1], slab.at[1], send_sem).wait()

    @pl.when(jnp.logical_not(is_mine))
    def _():
        pltpu.make_async_copy(slab, slab, send_sem).wait()


def body(
    pixels, row_mask, col_mask, route, tile, wcs_offset, subpixel, plate_scale, stretch_weight, psf_taps
):
    pix = pixels.reshape(NS, S, S)
    route = route.reshape(NS)
    tile = tile.reshape(NS)
    gain = stretch_weight.reshape(NS).astype(f32)
    scale = plate_scale.reshape(NS, 1, 1).astype(f32)
    shift = wcs_offset.reshape(NS, 2, 1).astype(f32) + subpixel.reshape(NS, 2, 1).astype(f32)
    grid_pos = jnp.arange(S).astype(f32)
    middle = S / 2.0
    source = scale * (grid_pos - middle) + (middle + shift)
    lowest = jnp.floor(source) - 2.0
    taps = jnp.arange(6).astype(f32)[None, None, :, None]
    factor = jnp.stack([jnp.ones_like(gain), gain], axis=1)[:, :, None, None]
    spots = lowest[:, :, None, :] + taps
    weights = (factor * lanczos(spots - source[:, :, None, :])).astype(bf16).astype(f32)
    masks = jnp.stack([row_mask.reshape(NS, S), col_mask.reshape(NS, S)], axis=1).astype(f32)
    wts = jnp.concatenate([weights, lowest[:, :, None], masks[:, :, None]], axis=2)
    wts = wts.reshape(NS, 16, S)
    kern = (psf_taps / jnp.sum(psf_taps, axis=2, keepdims=True)).astype(bf16).astype(f32)
    kern = kern.reshape(4, TAPS)

    order = jnp.arange(NS)
    rank = jnp.sum(
        (route[:, None] == route[None, :]) & (order[None, :] < order[:, None]), axis=1
    )
    line = jnp.arange(8 * NP)
    here = (route[None, :] == line[:, None] // 8) & (rank[None, :] == line[:, None] % 8 // 4)
    pp = (
        here[None] & ((line % 4)[None, :, None] == jnp.arange(4)[:, None, None])
    ).astype(bf16)
    slot_tile = jnp.sum(here * tile[None, :], axis=1).astype(f32)
    code = (route * 4 + tile).astype(f32)
    code_line = jnp.broadcast_to(code[None, :], (NP, 8)).reshape(8 * NP)
    extra = jnp.where(jnp.arange(128)[None, :] == 0, code_line[:, None], slot_tile[:, None])

    outer = outer_tables()
    outer_x = jnp.pad(outer.astype(f32), ((0, 0), (0, 112), (0, 0)))
    vm = pl.BlockSpec(memory_space=pltpu.VMEM)
    sm = pl.BlockSpec(memory_space=pltpu.SMEM)
    hbm = pl.BlockSpec(memory_space=pl.ANY)
    dma = pltpu.SemaphoreType.DMA
    recv, rfr, rsmall, moments, vmat = pl.pallas_call(
        warp_kernel,
        out_shape=(
            jax.ShapeDtypeStruct((NP, NS, ROWS, S), bf16),
            jax.ShapeDtypeStruct((NP, NS, ROWS, S), bf16),
            jax.ShapeDtypeStruct((NP, 8, 384), f32),
            jax.ShapeDtypeStruct((16, 128), f32),
            jax.ShapeDtypeStruct((2, 512, 256), bf16),
        ),
        in_specs=[sm, sm, sm, vm, vm, vm, vm, vm, vm],
        out_specs=(hbm, hbm, hbm, vm, vm),
        scratch_shapes=[
            pltpu.VMEM((NS, S, S), bf16),
            pltpu.VMEM((NS, ROWS, S), bf16),
            pltpu.VMEM((896, S), bf16),
            pltpu.VMEM((S, S), f32),
            pltpu.VMEM((S, S), bf16),
            pltpu.VMEM((2, 128, 256), bf16),
            pltpu.VMEM((8, 2 * S), f32),
            pltpu.VMEM((2, 16, S), f32),
            pltpu.VMEM((128, 384), f32),
            pltpu.VMEM((16, 128), f32),
            pltpu.VMEM((NV, 16, 128), f32),
            dma((NS,)), dma((NS,)), dma((NS,)), dma((NS,)),
            dma, dma, dma, dma,
        ],
        compiler_params=pltpu.CompilerParams(
            has_side_effects=True, vmem_limit_bytes=48 * 1024 * 1024
        ),
        name="warp_send",
    )(kern, tile // 2, gain, pix, wts, outer, outer_x, pp, extra)

    codes = rsmall[:, :, 256].reshape(NP * NS).astype(jnp.int32)
    slab = pl.pallas_call(
        layer_kernel,
        out_shape=jax.ShapeDtypeStruct((2, 64, ROWS, 256), bf16),
        in_specs=[sm, vm, hbm, vm],
        out_specs=vm,
        scratch_shapes=[
            pltpu.VMEM((2, 2, 66, ROWS, 256), f32),
            pltpu.VMEM((NP, NS, ROWS, S), bf16),
            dma,
        ],
        compiler_params=pltpu.CompilerParams(vmem_limit_bytes=48 * 1024 * 1024),
        name="layer_smooth",
    )(codes, recv, rfr, vmat)

    covers = rsmall[:, :, 0:256].reshape(2 * NP, 2 * S)
    tiles = rsmall[:, ::4, 257].reshape(1, 2 * NP, 1, 1).astype(jnp.int32)
    owner = jnp.arange(NV)[:, None, None, None]
    keep = (tiles // 2 == owner // 4) & (tiles % 2 == jnp.arange(2)[None, None, :, None])
    row_part = covers[:, :S].reshape(2 * NP, 4, 128).transpose(1, 0, 2)
    row_part = jnp.concatenate([row_part, row_part], axis=0)
    row_part = jnp.where(keep, row_part[:, :, None, :], 0.0).reshape(NV, 2 * NP, 256)
    col_part = jnp.broadcast_to(covers[None, :, S:], (NV, 2 * NP, S))
    wmsg = jnp.concatenate([col_part, row_part], axis=2).astype(bf16)

    flux, weight = pl.pallas_call(
        owner_kernel,
        out_shape=(
            jax.ShapeDtypeStruct((128, 2 * S), f32),
            jax.ShapeDtypeStruct((128, 2 * S), f32),
        ),
        in_specs=[vm, vm],
        out_specs=(vm, vm),
        scratch_shapes=[
            pltpu.VMEM((NV, 4, 4, ROWS, 256), bf16),
            pltpu.VMEM((NV, 2 * NP, 768), bf16),
            dma, dma, dma, dma,
        ],
        compiler_params=pltpu.CompilerParams(
            has_side_effects=True, vmem_limit_bytes=48 * 1024 * 1024
        ),
        name="owner_sum",
    )(slab, wmsg)

    norm_factor = 1.0 / (NV * 2 * 4 * S * S)
    first = np.array([pair[0] for pair in PAIRS])
    second = np.array([pair[1] for pair in PAIRS])
    pick_row = np.zeros((100, 16), np.float32)
    pick_col = np.zeros((100, 16), np.float32)
    for q in range(10):
        for r in range(10):
            pick_row[10 * q + r, 4 * first[q] + first[r]] = 1
            pick_col[10 * q + r, 4 * second[q] + second[r]] = 1
    picked = jnp.dot(pick_row, moments[:, :16], precision=precise)
    hessian = jnp.sum(picked * pick_col, axis=1).reshape(1, 10, 10) * norm_factor
    return flux, weight, hessian


def solution(mesh):
    in_specs = (
        P("patch", "visit", None, None, None),
        P("patch", "visit", None, None),
        P("patch", "visit", None, None),
        P("patch", "visit", None),
        P("patch", "visit", None),
        P("patch", "visit", None, None),
        P("patch", "visit", None, None),
        P("patch", "visit", None),
        P("patch", "visit", None),
        P("visit", None, None),
    )
    out_specs = (P("visit", "patch"), P("visit", "patch"), P("patch", None, None))
    return jax.shard_map(body, mesh=mesh, in_specs=in_specs, out_specs=out_specs, check_vma=False)
```

time: 927 us -> 181 us (0.20)
  the two profiles are of different devices: /device:TPU:29 before, /device:TPU:106 now
where the time goes in v1:
time: 181 us
  Pallas kernels  165 us (91%)
  local copies, waits for them, and re-layouts  10.3 us (6%)
  other arithmetic  4.84 us (3%)
    pallas_call x1, Pallas kernels, body(): pl.pallas_call(owner_kernel, out_shape=(jax.ShapeDtypeStruct((128, 2 * S)...  85.7 us
    pallas_call x1, Pallas kernels, body(): pl.pallas_call(warp_kernel, out_shape=(jax.ShapeDtypeStruct((NP, NS, ROWS...  68.6 us
    pallas_call x1, Pallas kernels, body(): pl.pallas_call(layer_kernel, out_shape=jax.ShapeDtypeStruct((2, 64, ROWS,...  10.3 us

profile of v1, /device:TPU:106, one launch (start us, length us, event | category | flops | bytes accessed | tf_op | source)
XLA Modules:
  0.0 180.8 jit_solution(17482673190321636181)
XLA Ops:
  0.7 0.8 eq.130
  1.4 0.8 reshape.700
  2.2 0.2 convert_reduce_fusion.2
  2.4 0.7 reshape.708
  3.1 0.7 convert_element_type.147
  3.9 0.7 reshape.707.gain
  4.7 0.8 fusion.3
  5.5 0.7 add_add_fusion
  6.8 0.2 select_reduce_fusion
  7.0 0.7 stack.25
  7.7 0.7 stack.26
  8.8 0.1 and_convert_fusion.pp
  9.0 0.7 fusion.34
  9.8 68.6 %warp_send.1 = (bf16[16,8,32,512]{3,2,1,0:T(8,128)(2,1)S(1)}, bf16[16,8,32,512]{3,2,1,0:T(8,128)(2,1)}, f32[16,8,384]{2,1,0:T(8,128)S(1)}, f32[16,128]{1,0:T(8,128)S(1)}, bf16[2,512,256]{2,1,0:T(8,128)(2,1)S(1)}) custom-call(f32[4,41]{1,0:T(4,128)S(1)} %convert.18.kern, s32[8]{0:T(128)S(1)} %get-tuple-element.42.trow, f32[8]{0:T(128)S(1)} %reshape.707.gain, ...), custom_call_target="tpu_custom_call" | custom-call | tf_op jit(solution)/shard_map/warp_send/pallas_call | solution.py:418
  78.4 2.0 %copy-done = bf16[16,8,32,512]{3,2,1,0:T(8,128)(2,1)} copy-done((bf16[16,8,32,512]{3,2,1,0:T(8,128)(2,1)}, bf16[16,8,32,512]{3,2,1,0:T(8,128)(2,1)S(1)}, u32[]{:S(2)}) %copy-start) | copy-done | bytes 4194328
  80.4 0.3 fusion.1
  80.7 0.7 mul.240
  81.3 0.3 convert_reduce_fusion
  81.8 10.3 %layer_smooth.1.slab = bf16[2,64,32,256]{3,2,1,0:T(8,128)(2,1)S(1)} custom-call(s32[128]{0:T(128)S(1)} %convert_element_type.165.codes, bf16[16,8,32,512]{3,2,1,0:T(8,128)(2,1)} %copy-done, bf16[16,8,32,512]{3,2,1,0:T(8,128)(2,1)} %get-tuple-element.13.rfr, bf16[2,512,256]{2,1,0:T(8,128)(2,1)S(1)} %get-tuple-element.14.vmat), custom_call_target="tpu_custom_call" | custom-call | tf_op jit(solution)/shard_map/layer_smooth/pallas_call | solution.py:451
  92.2 0.3 convert_reduce_fusion.1
  93.0 0.3 select_convert_fusion
  93.5 85.7 %owner_sum.1 = (f32[128,1024]{1,0:T(8,128)S(1)}, f32[128,1024]{1,0:T(8,128)S(1)}) custom-call(bf16[2,64,32,256]{3,2,1,0:T(8,128)(2,1)S(1)} %layer_smooth.1.slab, bf16[8,32,768]{2,1,0:T(8,128)(2,1)S(1)} %pad_maximum_fusion.wmsg), custom_call_target="tpu_custom_call" | custom-call | tf_op jit(solution)/shard_map/owner_sum/pallas_call | solution.py:475
  179.2 0.8 copy.56
  180.0 0.8 copy.57
  (51 shorter events, 1.8 us)
Async XLA Ops:
  0.6 79.8 %copy-start.2 = (f32[100,16]{0,1:T(8,128)S(1)}, f32[100,16]{0,1:T(8,128)}, u32[]{:S(2)}) copy-start(f32[100,16]{0,1:T(8,128)} %constant.174.clone) | copy-start | bytes 19204
  0.6 79.7 %copy-start.1 = (f32[100,16]{1,0:T(8,128)S(1)}, f32[100,16]{1,0:T(8,128)}, u32[]{:S(2)}) copy-start(f32[100,16]{1,0:T(8,128)} %constant.173.clone) | copy-start | bytes 19204
  78.4 2.0 %copy-start = (bf16[16,8,32,512]{3,2,1,0:T(8,128)(2,1)}, bf16[16,8,32,512]{3,2,1,0:T(8,128)(2,1)S(1)}, u32[]{:S(2)}) copy-start(bf16[16,8,32,512]{3,2,1,0:T(8,128)(2,1)S(1)} %get-tuple-element.12.recv) | copy-start | bytes 12582916

commit v2 on v1

--- a/solution.py
+++ b/solution.py
@@ -17,7 +17,7 @@
 NV = 8
 NS = 8
 ROWS = S // NP
-HOT = NP - 1
+SPILL = 10
 
 
 def lanczos(offset):
@@ -62,12 +62,14 @@
     return value
 
 
-def tap_matrix(kern, line, shape, shift):
-    at = (
-        lax.broadcasted_iota(jnp.int32, shape, 0)
-        - lax.broadcasted_iota(jnp.int32, shape, 1)
+def spill_row(row):
+    return 2 * (row // 16) + row % 2
+
+
+def tap_matrix(kern, line, shape, tap_of):
+    at = tap_of(
+        lax.broadcasted_iota(jnp.int32, shape, 0), lax.broadcasted_iota(jnp.int32, shape, 1)
     )
-    at = shift(at)
 
     def one(m, value):
         return jnp.where(at == m, kern[line, m], value)
@@ -76,9 +78,9 @@
 
 
 def warp_kernel(
-    kern, trow, gain, pix, wts, oy, ox, pp, extra,
+    kern, trow, gain, pix, wts, ylines, oy, ox, pp, extra,
     recv, rfr, rsmall, hess, vmat,
-    sbuf, fbuf, wpad, ybuf, half, umat, cov, rmom, small, msend, mrecv,
+    sbuf, fbuf, wpad, ybuf, half, edges, umat, cov, rmom, small, msend, mrecv,
     send_sem, recv_sem, fsend, frecv, ssend, srecv, msend_sem, mrecv_sem,
 ):
     me_v = lax.axis_index("visit")
@@ -87,11 +89,11 @@
     wpad[704:896, :] = jnp.zeros((192, S), bf16)
     rmom[...] = jnp.zeros_like(rmom)
     for v in range(2):
-        umat[v] = tap_matrix(kern, 2 * v + 1, (128, 256), lambda at: -at - 44).astype(bf16)
-
-    def stretch(s, carry):
+        line = jnp.broadcast_to(ylines[v : v + 1], (128, 256))
+        umat[v] = pltpu.roll(line, 0, 1, stride=1, stride_axis=0).astype(bf16)
+
+    def stretch(s):
         v = s // 4
-        piece = s % 4
         is_low = trow[s] == 0
         wt = wts[s]
         columns = jnp.transpose(wt[0:8])
@@ -119,17 +121,21 @@
         for a in range(4):
             ybuf[128 * a : 128 * a + 128, :] = dot(
                 umat[v], wpad[128 + 128 * a : 384 + 128 * a, :]
-            )
-        above = dot(umat[v, 96:128, :], wpad[0:256, :])
-        below = dot(umat[v, 0:32, :], wpad[640:896, :])
-        fbuf[s] = jnp.where(is_low, below, above).astype(bf16)
+            ).astype(bf16)
         for q in range(NP):
             low = ybuf[ROWS * q : ROWS * (q + 1), :]
             high = ybuf[ROWS * (NP - 1 - q) : ROWS * (NP - q), :]
-            sbuf[s, ROWS * q : ROWS * (q + 1), :] = jnp.where(is_low, low, high).astype(bf16)
+            sbuf[s, ROWS * q : ROWS * (q + 1), :] = jnp.where(is_low, low, high)
+        edges[s, 0:64] = wpad[192:256, :]
+        edges[s, 64:128] = wpad[640:704, :]
+
+    turn = 7 * me + 3 * me_v
+
+    def step(s, carry):
+        stretch(s)
 
         def send(j, carry):
-            k = lax.rem(me + j, NP)
+            k = lax.rem(me + 1 + lax.rem(turn + j, NP - 1), NP)
             pltpu.make_async_remote_copy(
                 src_ref=sbuf.at[s, pl.ds(pl.multiple_of(k * ROWS, ROWS), ROWS)],
                 dst_ref=recv.at[me, s],
@@ -140,34 +146,62 @@
             ).start()
             return carry
 
-        lax.fori_loop(1, NP, send, 0)
+        lax.fori_loop(0, NP - 1, send, 0)
         pltpu.make_async_copy(
             sbuf.at[s, pl.ds(pl.multiple_of(me * ROWS, ROWS), ROWS)], recv.at[me, s], recv_sem.at[s]
         ).start()
-
-        @pl.when(me != HOT)
+        return carry
+
+    lax.fori_loop(0, NS, step, 0)
+
+    row = lax.broadcasted_iota(jnp.int32, (16 * SPILL, 128), 0)
+    lane = lax.broadcasted_iota(jnp.int32, (16 * SPILL, 128), 1)
+    spilled = jnp.zeros((16 * SPILL, S), f32)
+    for v in range(2):
+        taps = tap_matrix(
+            kern,
+            2 * v + 1,
+            (16 * SPILL, 128),
+            lambda row, lane: jnp.where(
+                lane >= 64, lane - spill_row(row) - 108, lane + spill_row(row) + 21
+            ),
+        )
+        for s in range(4 * v, 4 * v + 4):
+            keep = (row % 16 // 2 == s) & (lane // 64 == 1 - trow[s])
+            spilled += dot(jnp.where(keep, taps, 0.0).astype(bf16), edges[s])
+    fbuf[...] = spilled.astype(bf16)
+
+    def send_spill(k, carry):
+        src = fbuf.at[pl.ds(pl.multiple_of(16 * k, 16), 16)]
+
+        @pl.when(me != k)
         def _():
             pltpu.make_async_remote_copy(
-                src_ref=fbuf.at[s],
-                dst_ref=rfr.at[me, s],
-                send_sem=fsend.at[s],
-                recv_sem=frecv.at[s],
-                device_id={"patch": HOT},
+                src_ref=src,
+                dst_ref=rfr.at[me],
+                send_sem=fsend,
+                recv_sem=frecv,
+                device_id={"patch": k},
                 device_id_type=MESH,
             ).start()
 
-        @pl.when(me == HOT)
+        @pl.when(me == k)
         def _():
-            pltpu.make_async_copy(fbuf.at[s], rfr.at[me, s], frecv.at[s]).start()
-
+            pltpu.make_async_copy(src, rfr.at[me], frecv).start()
+
+        return carry
+
+    lax.fori_loop(0, SPILL, send_spill, 0)
+
+    def moments(s, carry):
+        piece = s % 4
         values = pix[s].astype(f32)
         square = (values * values).astype(bf16)
-        lhs = oy[piece // 2] * row_mask.astype(bf16)
-        rmom[piece % 2] += dot(lhs, square) * (col_mask * gain[s])
-        return carry
-
-    lax.fori_loop(0, NS, stretch, 0)
-
+        lhs = oy[piece // 2] * wts[s, 7:8].astype(bf16)
+        rmom[piece % 2] += dot(lhs, square) * (wts[s, 15:16] * gain[s])
+        return carry
+
+    lax.fori_loop(0, NS, moments, 0)
     covers = cov[...].astype(bf16)
     slots = dot(pp[0], covers[:, 0:256])
     for b in range(1, 4):
@@ -210,7 +244,7 @@
     for v in range(2):
         for c in range(4):
             vmat[v, 128 * c : 128 * c + 128, :] = tap_matrix(
-                kern, 2 * v, (128, 256), lambda at: at + (128 * c - 108)
+                kern, 2 * v, (128, 256), lambda row, lane: row - lane + (128 * c - 108)
             ).astype(bf16)
 
     pltpu.make_async_copy(mrecv, mrecv, mrecv_sem).wait()
@@ -222,26 +256,27 @@
     pltpu.make_async_copy(rsmall, rsmall, srecv).wait()
     pltpu.make_async_copy(rsmall.at[1:NP], rsmall.at[1:NP], ssend).wait()
 
-    def finish(s, carry):
-        everyone = recv.at[:, s]
-        others = recv.at[1:NP, s]
-        pltpu.make_async_copy(everyone, everyone, recv_sem.at[s]).wait()
-        pltpu.make_async_copy(others, others, send_sem.at[s]).wait()
-
-        @pl.when(me != HOT)
-        def _():
-            pltpu.make_async_copy(fbuf.at[s], fbuf.at[s], fsend.at[s]).wait()
-
-        @pl.when(me == HOT)
-        def _():
-            pltpu.make_async_copy(rfr.at[:, s], rfr.at[:, s], frecv.at[s]).wait()
-
+    def finish(i, carry):
+        everyone = recv.at[:, i]
+        others = recv.at[1:NP, i]
+        pltpu.make_async_copy(everyone, everyone, recv_sem.at[i]).wait()
+        pltpu.make_async_copy(others, others, send_sem.at[i]).wait()
         return carry
 
     lax.fori_loop(0, NS, finish, 0)
 
-
-def layer_kernel(codes, recv, rfr, vmat, out, acc, fvm, sem):
+    @pl.when(me < SPILL)
+    def _():
+        others = fbuf.at[0 : 16 * (SPILL - 1)]
+        pltpu.make_async_copy(rfr, rfr, frecv).wait()
+        pltpu.make_async_copy(others, others, fsend).wait()
+
+    @pl.when(me >= SPILL)
+    def _():
+        pltpu.make_async_copy(fbuf, fbuf, fsend).wait()
+
+
+def layer_kernel(codes, recv, rfr, vmat, out, outf, acc, accf, fvm, sem):
     me = lax.axis_index("patch")
     zero = jnp.zeros((ROWS, 256), f32)
 
@@ -253,84 +288,116 @@
 
     lax.fori_loop(0, 66, clear, 0)
 
-    def place(at, s, value, flip):
+    def add(at, carry):
+        s = at % NS
         code = codes[at]
         tile = code % 4
         g = 2 * (code // 4) + tile % 2
         t = tile // 2
-        if flip:
-            t = 1 - t
-        data = value.astype(f32)
+        data = recv[at // NS, s].astype(f32)
         acc[s // 4, t, 2 * g + 1] += data[:, 0:256]
         acc[s // 4, t, 2 * g + 2] += data[:, 256:512]
-
-    def add(at, carry):
-        s = at % NS
-        place(at, s, recv[at // NS, s], False)
         return carry
 
     lax.fori_loop(0, NP * NS, add, 0)
 
-    @pl.when(me == HOT)
+    def smooth(blocks_of, count):
+        total = None
+        rows = blocks_of(0).shape[0] // (count + 2)
+        for v in range(2):
+            block = blocks_of(v)
+            part = dot(block[rows : (count + 1) * rows], vmat[v, 128:384])
+            part += dot(block[0 : count * rows, 128:256], vmat[v, 0:128])
+            part += dot(block[2 * rows : (count + 2) * rows, 0:128], vmat[v, 384:512])
+            total = part if total is None else total + part
+        return total.astype(bf16)
+
+    for t in range(2):
+        for c in range(4):
+            total = smooth(
+                lambda v: acc[v, t, 16 * c : 16 * c + 18].reshape(18 * ROWS, 256).astype(bf16), 16
+            )
+            out[t, 16 * c : 16 * c + 16] = total.reshape(16, ROWS, 256)
+
+    @pl.when(me < SPILL)
     def _():
         copy = pltpu.make_async_copy(rfr, fvm, sem)
         copy.start()
+        accf[...] = jnp.zeros_like(accf)
         copy.wait()
-
-        def add_fringe(at, carry):
-            s = at % NS
-            place(at, s, fvm[at // NS, s], True)
+        target = lax.broadcasted_iota(jnp.int32, (8, S), 0) // 2
+
+        def add_spill(c, carry):
+            rows = fvm[c].astype(f32)
+            for s in range(NS):
+                code = codes[c * NS + s]
+                tile = code % 4
+                g = 2 * (code // 4) + tile % 2
+                two = rows[2 * s : 2 * s + 2]
+                data = jnp.where(
+                    target == 1 - tile // 2, jnp.concatenate([two, two, two, two], axis=0), 0.0
+                )
+                accf[s // 4, 2 * g + 1] += data[:, 0:256]
+                accf[s // 4, 2 * g + 2] += data[:, 256:512]
             return carry
 
-        lax.fori_loop(0, NP * NS, add_fringe, 0)
-
-    for t in range(2):
-        for c in range(4):
-            total = None
-            for v in range(2):
-                block = acc[v, t, 16 * c : 16 * c + 18].reshape(18 * ROWS, 256).astype(bf16)
-                left = block[0 : 16 * ROWS, 128:256]
-                middle = block[ROWS : 17 * ROWS]
-                right = block[2 * ROWS : 18 * ROWS, 0:128]
-                part = dot(middle, vmat[v, 128:384])
-                part += dot(left, vmat[v, 0:128])
-                part += dot(right, vmat[v, 384:512])
-                total = part if total is None else total + part
-            out[t, 16 * c : 16 * c + 16] = total.astype(bf16).reshape(16, ROWS, 256)
-
-
-def owner_kernel(slab, wmsg, flux, weight, frecv, wrecv, send_sem, recv_sem, wsend_sem, wrecv_sem):
+        lax.fori_loop(0, NP, add_spill, 0)
+        outf[...] = smooth(lambda v: accf[v].reshape(66 * 8, 256).astype(bf16), 64)
+
+
+def owner_kernel(
+    slab, spill, wmsg, flux, weight,
+    part, summed, frecv, wrecv, spart, ssum, srecv,
+    part_send, part_recv, sum_send, sum_recv, wsend_sem, wrecv_sem,
+    spart_send, spart_recv, ssum_send, ssum_recv,
+):
     me_v = lax.axis_index("visit")
     me = lax.axis_index("patch")
+
+    turn = 3 * me_v + 2 * me
+
+    def group(v):
+        return lax.rem(v + me // 2, NV)
+
+    mine_group = group(me_v)
+
     for t in range(2):
-        block = me if t == 0 else NP - 1 - me
-        r = 4 * t + block // 4
-        slot = lax.rem(block, 4)
-
-        def send(j, carry):
-            p = lax.rem(me + j, NP)
-            src = slab.at[t, pl.ds(4 * p, 4)]
-            dst = frecv.at[me_v, slot]
-            mine = (r == me_v) & (p == me)
-
-            @pl.when(jnp.logical_not(mine))
-            def _():
-                pltpu.make_async_remote_copy(
-                    src_ref=src,
-                    dst_ref=dst,
-                    send_sem=send_sem,
-                    recv_sem=recv_sem,
-                    device_id={"visit": r, "patch": p},
-                    device_id_type=MESH,
-                ).start()
-
-            @pl.when(mine)
-            def _():
-                pltpu.make_async_copy(src, dst, recv_sem).start()
-
+
+        def send_part(j, carry):
+            r = lax.rem(me_v + 1 + lax.rem(turn + j, NV - 1), NV)
+            pltpu.make_async_remote_copy(
+                src_ref=slab.at[t, pl.ds(8 * group(r), 8)],
+                dst_ref=part.at[t, me_v],
+                send_sem=part_send.at[t],
+                recv_sem=part_recv.at[t],
+                device_id={"visit": r},
+                device_id_type=MESH,
+            ).start()
             return carry
 
-        lax.fori_loop(0, NP, send, 0)
+        lax.fori_loop(0, NV - 1, send_part, 0)
+        pltpu.make_async_copy(
+            slab.at[t, pl.ds(8 * mine_group, 8)], part.at[t, me_v], part_recv.at[t]
+        ).start()
+
+    @pl.when(me < SPILL)
+    def _():
+        def send_spill(j, carry):
+            r = lax.rem(me_v + j, NV)
+            pltpu.make_async_remote_copy(
+                src_ref=spill.at[pl.ds(pl.multiple_of(64 * group(r), 64), 64)],
+                dst_ref=spart.at[me_v],
+                send_sem=spart_send,
+                recv_sem=spart_recv,
+                device_id={"visit": r},
+                device_id_type=MESH,
+            ).start()
+            return carry
+
+        lax.fori_loop(1, NV, send_spill, 0)
+        pltpu.make_async_copy(
+            spill.at[pl.ds(pl.multiple_of(64 * mine_group, 64), 64)], spart.at[me_v], spart_recv
+        ).start()
 
     def send_weight(j, carry):
         r = lax.rem(me_v + j, NV)
@@ -346,30 +413,122 @@
 
     lax.fori_loop(1, NV, send_weight, 0)
     pltpu.make_async_copy(wmsg.at[me_v], wrecv.at[me_v], wrecv_sem).start()
+
+    for t in range(2):
+        block = me if t == 0 else NP - 1 - me
+        r = 4 * t + block // 4
+        slot = lax.rem(block, 4)
+        pltpu.make_async_copy(part.at[t], part.at[t], part_recv.at[t]).wait()
+
+        def add(b, carry):
+            total = part[t, 0, b].astype(f32)
+            for v in range(1, NV):
+                total += part[t, v, b].astype(f32)
+            summed[t, b] = total.astype(bf16)
+            return carry
+
+        lax.fori_loop(0, 8, add, 0)
+        for half in range(2):
+            p = 2 * mine_group + half
+            mine = (r == me_v) & (p == me)
+            src = summed.at[t, 4 * half : 4 * half + 4]
+
+            @pl.when(jnp.logical_not(mine))
+            def _():
+                pltpu.make_async_remote_copy(
+                    src_ref=src,
+                    dst_ref=frecv.at[slot],
+                    send_sem=sum_send.at[t, half],
+                    recv_sem=sum_recv,
+                    device_id={"visit": r, "patch": p},
+                    device_id_type=MESH,
+                ).start()
+
+            @pl.when(mine)
+            def _():
+                pltpu.make_async_copy(src, frecv.at[slot], sum_recv).start()
+
+    def spill_legs(act):
+        for half in range(2):
+            for t in range(2):
+                act(half, t, (me_v == 3 + t) & (me == 2 * mine_group + half))
+
+    @pl.when(me < SPILL)
+    def _():
+        pltpu.make_async_copy(spart, spart, spart_recv).wait()
+        total = spart[0].astype(f32)
+        for v in range(1, NV):
+            total += spart[v].astype(f32)
+        ssum[...] = total
+
+        def leg(half, t, mine):
+            src = ssum.at[32 * half : 32 * half + 32]
+
+            @pl.when(jnp.logical_not(mine))
+            def _():
+                pltpu.make_async_remote_copy(
+                    src_ref=src,
+                    dst_ref=srecv.at[me],
+                    send_sem=ssum_send.at[t, half],
+                    recv_sem=ssum_recv,
+                    device_id={"visit": 3 + t, "patch": 2 * mine_group + half},
+                    device_id_type=MESH,
+                ).start()
+
+            @pl.when(mine)
+            def _():
+                pltpu.make_async_copy(src, srecv.at[me], ssum_recv).start()
+
+        spill_legs(leg)
+
     pltpu.make_async_copy(wrecv, wrecv, wrecv_sem).wait()
     cols = wrecv[:, :, 0:512].reshape(NV * 2 * NP, 512)
     left = wrecv[:, :, 512:640].reshape(NV * 2 * NP, 128)
     right = wrecv[:, :, 640:768].reshape(NV * 2 * NP, 128)
     weight[:, 0:512] = dot_tn(left, cols)
     weight[:, 512:1024] = dot_tn(right, cols)
-    pltpu.make_async_copy(frecv, frecv, recv_sem).wait()
+    pltpu.make_async_copy(frecv, frecv, sum_recv).wait()
     for slot in range(4):
         for q in range(4):
-            total = frecv[0, slot, q].astype(f32)
-            for v in range(1, NV):
-                total += frecv[v, slot, q].astype(f32)
-            flux[32 * slot : 32 * slot + 32, 256 * q : 256 * q + 256] = total
+            flux[32 * slot : 32 * slot + 32, 256 * q : 256 * q + 256] = frecv[slot, q].astype(f32)
+    for t in range(2):
+
+        @pl.when(me_v == 3 + t)
+        def _():
+            pltpu.make_async_copy(srecv, srecv, ssum_recv).wait()
+            for k in range(SPILL):
+                for e in range(2):
+                    at = 2 * k + e
+                    line = at if t == 1 else 127 - at
+                    for q in range(4):
+                        flux[line : line + 1, 256 * q : 256 * q + 256] += srecv[
+                            k, 8 * q + 2 * t + e : 8 * q + 2 * t + e + 1, :
+                        ]
+
+    @pl.when(me < SPILL)
+    def _():
+        pltpu.make_async_copy(spart.at[1:NV], spart.at[1:NV], spart_send).wait()
+
+        def leg_sent(half, t, mine):
+            @pl.when(jnp.logical_not(mine))
+            def _():
+                src = ssum.at[32 * half : 32 * half + 32]
+                pltpu.make_async_copy(src, src, ssum_send.at[t, half]).wait()
+
+        spill_legs(leg_sent)
+
     pltpu.make_async_copy(wrecv.at[1:NV], wrecv.at[1:NV], wsend_sem).wait()
-    is_mine = (me_v == me // 4) | (me_v == 4 + (NP - 1 - me) // 4)
-
-    @pl.when(is_mine)
-    def _():
-        pltpu.make_async_copy(slab.at[0, 0:60], slab.at[0, 0:60], send_sem).wait()
-        pltpu.make_async_copy(slab.at[1], slab.at[1], send_sem).wait()
-
-    @pl.when(jnp.logical_not(is_mine))
-    def _():
-        pltpu.make_async_copy(slab, slab, send_sem).wait()
+    for t in range(2):
+        block = me if t == 0 else NP - 1 - me
+        r = 4 * t + block // 4
+        pltpu.make_async_copy(part.at[t, 1:NV], part.at[t, 1:NV], part_send.at[t]).wait()
+        for half in range(2):
+            mine = (r == me_v) & (2 * mine_group + half == me)
+
+            @pl.when(jnp.logical_not(mine))
+            def _():
+                src = summed.at[t, 4 * half : 4 * half + 4]
+                pltpu.make_async_copy(src, src, sum_send.at[t, half]).wait()
 
 
 def body(
@@ -393,6 +552,7 @@
     wts = jnp.concatenate([weights, lowest[:, :, None], masks[:, :, None]], axis=2)
     wts = wts.reshape(NS, 16, S)
     kern = (psf_taps / jnp.sum(psf_taps, axis=2, keepdims=True)).astype(bf16).astype(f32)
+    ylines = jnp.pad(kern[:, 1], ((0, 0), (44, 256 - 44 - TAPS)))
     kern = kern.reshape(4, TAPS)
 
     order = jnp.arange(NS)
@@ -419,43 +579,48 @@
         warp_kernel,
         out_shape=(
             jax.ShapeDtypeStruct((NP, NS, ROWS, S), bf16),
-            jax.ShapeDtypeStruct((NP, NS, ROWS, S), bf16),
+            jax.ShapeDtypeStruct((NP, 16, S), bf16),
             jax.ShapeDtypeStruct((NP, 8, 384), f32),
             jax.ShapeDtypeStruct((16, 128), f32),
             jax.ShapeDtypeStruct((2, 512, 256), bf16),
         ),
-        in_specs=[sm, sm, sm, vm, vm, vm, vm, vm, vm],
+        in_specs=[sm, sm, sm, vm, vm, vm, vm, vm, vm, vm],
         out_specs=(hbm, hbm, hbm, vm, vm),
         scratch_shapes=[
             pltpu.VMEM((NS, S, S), bf16),
-            pltpu.VMEM((NS, ROWS, S), bf16),
+            pltpu.VMEM((16 * SPILL, S), bf16),
             pltpu.VMEM((896, S), bf16),
-            pltpu.VMEM((S, S), f32),
             pltpu.VMEM((S, S), bf16),
+            pltpu.VMEM((S, S), bf16),
+            pltpu.VMEM((NS, 128, S), bf16),
             pltpu.VMEM((2, 128, 256), bf16),
             pltpu.VMEM((8, 2 * S), f32),
             pltpu.VMEM((2, 16, S), f32),
             pltpu.VMEM((128, 384), f32),
             pltpu.VMEM((16, 128), f32),
             pltpu.VMEM((NV, 16, 128), f32),
-            dma((NS,)), dma((NS,)), dma((NS,)), dma((NS,)),
-            dma, dma, dma, dma,
+            dma((NS,)), dma((NS,)),
+            dma, dma, dma, dma, dma, dma,
         ],
         compiler_params=pltpu.CompilerParams(
             has_side_effects=True, vmem_limit_bytes=48 * 1024 * 1024
         ),
         name="warp_send",
-    )(kern, tile // 2, gain, pix, wts, outer, outer_x, pp, extra)
+    )(kern, tile // 2, gain, pix, wts, ylines, outer, outer_x, pp, extra)
 
     codes = rsmall[:, :, 256].reshape(NP * NS).astype(jnp.int32)
-    slab = pl.pallas_call(
+    slab, spill = pl.pallas_call(
         layer_kernel,
-        out_shape=jax.ShapeDtypeStruct((2, 64, ROWS, 256), bf16),
+        out_shape=(
+            jax.ShapeDtypeStruct((2, 64, ROWS, 256), bf16),
+            jax.ShapeDtypeStruct((512, 256), bf16),
+        ),
         in_specs=[sm, vm, hbm, vm],
-        out_specs=vm,
+        out_specs=(vm, vm),
         scratch_shapes=[
             pltpu.VMEM((2, 2, 66, ROWS, 256), f32),
-            pltpu.VMEM((NP, NS, ROWS, S), bf16),
+            pltpu.VMEM((2, 66, 8, 256), f32),
+            pltpu.VMEM((NP, 16, S), bf16),
             dma,
         ],
         compiler_params=pltpu.CompilerParams(vmem_limit_bytes=48 * 1024 * 1024),
@@ -478,18 +643,24 @@
             jax.ShapeDtypeStruct((128, 2 * S), f32),
             jax.ShapeDtypeStruct((128, 2 * S), f32),
         ),
-        in_specs=[vm, vm],
+        in_specs=[vm, vm, vm],
         out_specs=(vm, vm),
         scratch_shapes=[
-            pltpu.VMEM((NV, 4, 4, ROWS, 256), bf16),
+            pltpu.VMEM((2, NV, 8, ROWS, 256), bf16),
+            pltpu.VMEM((2, 8, ROWS, 256), bf16),
+            pltpu.VMEM((4, 4, ROWS, 256), bf16),
             pltpu.VMEM((NV, 2 * NP, 768), bf16),
-            dma, dma, dma, dma,
+            pltpu.VMEM((NV, 64, 256), bf16),
+            pltpu.VMEM((64, 256), f32),
+            pltpu.VMEM((SPILL, 32, 256), f32),
+            dma((2,)), dma((2,)), dma((2, 2)), dma, dma, dma,
+            dma, dma, dma((2, 2)), dma,
         ],
         compiler_params=pltpu.CompilerParams(
             has_side_effects=True, vmem_limit_bytes=48 * 1024 * 1024
         ),
         name="owner_sum",
-    )(slab, wmsg)
+    )(slab, spill, wmsg)
 
     norm_factor = 1.0 / (NV * 2 * 4 * S * S)
     first = np.array([pair[0] for pair in PAIRS])

time: 181 us -> 151 us (0.83)
  the two profiles are of different devices: /device:TPU:106 before, /device:TPU:29 now
where the time goes in v2:
time: 151 us; the launch traced here: 149 us
  Pallas kernels  132 us (87%)
  local copies, waits for them, and re-layouts  10.3 us (7%)
  other arithmetic  4.84 us (3%)
    pallas_call x1, Pallas kernels, body(): pl.pallas_call(warp_kernel, out_shape=(jax.ShapeDtypeStruct((NP, NS, ROWS...  69.2 us
    pallas_call x1, Pallas kernels, body(): pl.pallas_call(owner_kernel, out_shape=(jax.ShapeDtypeStruct((128, 2 * S)...  52.9 us
    pallas_call x1, Pallas kernels, body(): pl.pallas_call(layer_kernel, out_shape=(jax.ShapeDtypeStruct((2, 64, ROWS...  10.3 us
    unnamed x8, local copies, waits for them, and re-layouts  3.52 us

profile of v2, /device:TPU:29, one launch (start us, length us, event | category | flops | bytes accessed | tf_op | source)
XLA Modules:
  0.0 148.7 jit_solution(2631711858889752272)
XLA Ops:
  0.7 0.8 eq.130
  1.4 0.8 reshape.697
  2.2 0.2 convert_reduce_fusion.2
  2.4 0.7 reshape.703
  3.1 0.7 convert_element_type.152
  3.9 0.7 reshape.702.gain
  4.7 0.8 fusion.4
  5.6 0.7 add_add_fusion
  6.8 0.2 select_reduce_fusion
  7.1 0.7 stack.25
  7.8 0.7 stack.26
  8.9 0.1 and_convert_fusion.pp
  9.1 0.7 fusion.35
  9.9 69.2 %warp_send.1 = (bf16[16,8,32,512]{3,2,1,0:T(8,128)(2,1)S(1)}, bf16[16,16,512]{2,1,0:T(8,128)(2,1)S(1)}, f32[16,8,384]{2,1,0:T(8,128)S(1)}, f32[16,128]{1,0:T(8,128)S(1)}, bf16[2,512,256]{2,1,0:T(8,128)(2,1)S(1)}) custom-call(f32[4,41]{1,0:T(4,128)S(1)} %bitcast.17, s32[8]{0:T(128)S(1)} %get-tuple-element.46.trow, f32[8]{0:T(128)S(1)} %reshape.702.gain, ...), custom_call_target="tpu_custom_call" | custom-call | tf_op jit(solution)/shard_map/warp_send/pallas_call | solution.py:578
  79.1 1.9 %copy-done = bf16[16,8,32,512]{3,2,1,0:T(8,128)(2,1)} copy-done((bf16[16,8,32,512]{3,2,1,0:T(8,128)(2,1)}, bf16[16,8,32,512]{3,2,1,0:T(8,128)(2,1)S(1)}, u32[]{:S(2)}) %copy-start) | copy-done | bytes 4194328
  81.0 0.3 fusion.1
  81.3 0.7 mul.240
  82.0 0.3 convert_reduce_fusion
  82.4 10.3 %layer_smooth.1 = (bf16[2,64,32,256]{3,2,1,0:T(8,128)(2,1)S(1)}, bf16[512,256]{1,0:T(8,128)(2,1)S(1)}) custom-call(s32[128]{0:T(128)S(1)} %convert_element_type.170.codes, bf16[16,8,32,512]{3,2,1,0:T(8,128)(2,1)} %copy-done, bf16[16,16,512]{2,1,0:T(8,128)(2,1)S(1)} %get-tuple-element.15.rfr, bf16[2,512,256]{2,1,0:T(8,128)(2,1)S(1)} %get-tuple-element.16.vmat), custom_call_target="tpu_custom_call" | custom-call | tf_op jit(solution)/shard_map/layer_smooth/pallas_call | solution.py:612
  92.8 0.3 convert_reduce_fusion.1
  93.7 0.3 select_convert_fusion
  94.2 52.9 %owner_sum.1 = (f32[128,1024]{1,0:T(8,128)S(1)}, f32[128,1024]{1,0:T(8,128)S(1)}) custom-call(bf16[2,64,32,256]{3,2,1,0:T(8,128)(2,1)S(1)} %get-tuple-element.17.slab, bf16[512,256]{1,0:T(8,128)(2,1)S(1)} %get-tuple-element.18.spill, bf16[8,32,768]{2,1,0:T(8,128)(2,1)S(1)} %pad_maximum_fusion.wmsg), custom_call_target="tpu_custom_call" | custom-call | tf_op jit(solution)/shard_map/owner_sum/pallas_call | solution.py:640
  147.1 0.8 copy.56
  147.9 0.8 copy.57
  (52 shorter events, 1.9 us)
Async XLA Ops:
  0.6 80.4 %copy-start.2 = (f32[100,16]{0,1:T(8,128)S(1)}, f32[100,16]{0,1:T(8,128)}, u32[]{:S(2)}) copy-start(f32[100,16]{0,1:T(8,128)} %constant.174.clone) | copy-start | bytes 19204
  0.6 80.4 %copy-start.1 = (f32[100,16]{1,0:T(8,128)S(1)}, f32[100,16]{1,0:T(8,128)}, u32[]{:S(2)}) copy-start(f32[100,16]{1,0:T(8,128)} %constant.173.clone) | copy-start | bytes 19204
  79.1 1.9 %copy-start = (bf16[16,8,32,512]{3,2,1,0:T(8,128)(2,1)}, bf16[16,8,32,512]{3,2,1,0:T(8,128)(2,1)S(1)}, u32[]{:S(2)}) copy-start(bf16[16,8,32,512]{3,2,1,0:T(8,128)(2,1)S(1)} %get-tuple-element.14.recv) | copy-start | bytes 12582916

commit v3 on v2

--- a/solution.py
+++ b/solution.py
@@ -21,22 +21,30 @@
 
 
 def lanczos(offset):
-    inside = jnp.abs(offset) < 3.0
-    return jnp.where(inside, jnp.sinc(offset) * jnp.sinc(offset / 3.0), jnp.zeros_like(offset))
-
-
-def legendre(coord):
+    wide = offset * np.float32(np.pi)
+    narrow = wide * np.float32(1.0 / 3.0)
+    product = wide * narrow
+    ratio = jnp.sin(wide) * jnp.sin(narrow) / jnp.where(product == 0.0, 1.0, product)
+    value = jnp.where(product == 0.0, 1.0, ratio)
+    return jnp.where(jnp.abs(offset) < 3.0, value, 0.0)
+
+
+def outer_tables():
+    grid_pos = np.arange(S, dtype=np.float32)
+    block = np.arange(2, dtype=np.float32)
+    coord = (block[:, None] * np.float32(S) + grid_pos[None, :] + np.float32(0.5)) / np.float32(
+        S
+    ) - np.float32(1.0)
     square = coord * coord
-    return jnp.stack(
-        [jnp.ones_like(coord), coord, 1.5 * square - 0.5, (2.5 * square - 1.5) * coord], axis=-2
+    poly = np.stack(
+        [
+            np.ones_like(coord),
+            coord,
+            np.float32(1.5) * square - np.float32(0.5),
+            (np.float32(2.5) * square - np.float32(1.5)) * coord,
+        ],
+        axis=1,
     )
-
-
-def outer_tables():
-    grid_pos = jnp.arange(S).astype(f32)
-    block = jnp.arange(2).astype(f32)
-    coord = (block[:, None] * S + grid_pos[None, :] + 0.5) / S - 1.0
-    poly = legendre(coord)
     return (poly[:, :, None, :] * poly[:, None, :, :]).reshape(2, 16, S).astype(bf16)
 
 
@@ -66,39 +74,58 @@
     return 2 * (row // 16) + row % 2
 
 
-def tap_matrix(kern, line, shape, tap_of):
-    at = tap_of(
-        lax.broadcasted_iota(jnp.int32, shape, 0), lax.broadcasted_iota(jnp.int32, shape, 1)
+def sheared(line, rows):
+    return pltpu.roll(
+        jnp.broadcast_to(line, (rows, line.shape[1])), 0, 1, stride=1, stride_axis=0
     )
 
-    def one(m, value):
-        return jnp.where(at == m, kern[line, m], value)
-
-    return lax.fori_loop(0, TAPS, one, jnp.zeros(shape, f32))
-
 
 def warp_kernel(
-    kern, trow, gain, pix, wts, ylines, oy, ox, pp, extra,
+    params, route, tile, pix, row_masks, col_masks, psf, oy, ox,
     recv, rfr, rsmall, hess, vmat,
-    sbuf, fbuf, wpad, ybuf, half, edges, umat, cov, rmom, small, msend, mrecv,
-    send_sem, recv_sem, fsend, frecv, ssend, srecv, msend_sem, mrecv_sem,
+    sbuf, fbuf, wpad, ybuf, half, edges, umat, cov, rmom, small,
+    send_sem, recv_sem, fsend, frecv, ssend, srecv,
 ):
     me_v = lax.axis_index("visit")
     me = lax.axis_index("patch")
+    barrier = pltpu.get_barrier_semaphore()
+
+    def greet(j, carry):
+        pl.semaphore_signal(
+            barrier, inc=1, device_id={"patch": lax.rem(me + j, NP)}, device_id_type=MESH
+        )
+        return carry
+
+    lax.fori_loop(1, NP, greet, 0)
+    pl.semaphore_wait(barrier, NP - 1)
     wpad[0:192, :] = jnp.zeros((192, S), bf16)
     wpad[704:896, :] = jnp.zeros((192, S), bf16)
     rmom[...] = jnp.zeros_like(rmom)
+    tap_lines = []
     for v in range(2):
-        line = jnp.broadcast_to(ylines[v : v + 1], (128, 256))
-        umat[v] = pltpu.roll(line, 0, 1, stride=1, stride_axis=0).astype(bf16)
+        lines = psf[v] / jnp.sum(psf[v], axis=1, keepdims=True)
+        lines = lines.astype(bf16).astype(f32)
+        tap_lines.append(lines)
+        umat[v] = sheared(lines[1:2], 128).astype(bf16)
 
     def stretch(s):
         v = s // 4
-        is_low = trow[s] == 0
-        wt = wts[s]
-        columns = jnp.transpose(wt[0:8])
-        row_mask = wt[7:8]
-        col_mask = wt[15:16]
+        piece = s % 4
+        is_low = tile[0, v, piece] < 2
+        spot = lax.broadcasted_iota(jnp.int32, (8, S), 1).astype(f32) - 256.0
+        tap = lax.broadcasted_iota(jnp.int32, (8, S), 0).astype(f32)
+
+        def weights_along(axis, factor):
+            shift = params[0, v, piece, 1 + axis] + params[0, v, piece, 3 + axis]
+            source = params[0, v, piece, 0] * spot + (256.0 + shift)
+            lowest = jnp.floor(source) - 2.0
+            value = (factor * lanczos((lowest + tap) - source)).astype(bf16).astype(f32)
+            return jnp.where(tap == 6.0, lowest, value)
+
+        columns = jnp.transpose(weights_along(0, 1.0))
+        wt = weights_along(1, params[0, v, piece, 5])
+        row_mask = row_masks[0, v, pl.ds(piece, 1), :].astype(f32)
+        col_mask = col_masks[0, v, pl.ds(piece, 1), :].astype(f32)
         ones = jnp.ones((8, 384), bf16)
         for a in range(2):
             at = lax.broadcasted_iota(jnp.int32, (256, 384), 1).astype(f32) + float(128 * a)
@@ -112,7 +139,7 @@
         for b in range(2):
             at = lax.broadcasted_iota(jnp.int32, (384, 256), 0).astype(f32) + float(128 * b)
             lanes = wt[:, 256 * b : 256 * b + 256]
-            cols_map = band(at, lanes[14:15], lambda k: lanes[8 + k : 9 + k]).astype(bf16)
+            cols_map = band(at, lanes[6:7], lambda k: lanes[k : k + 1]).astype(bf16)
             part = dot(half[:, 128 * b : 128 * b + 384], cols_map)
             wpad[192:704, 256 * b : 256 * b + 256] = part.astype(bf16)
             mask = jnp.broadcast_to(col_mask[:, 128 * b : 128 * b + 384], (8, 384)).astype(bf16)
@@ -157,17 +184,17 @@
     row = lax.broadcasted_iota(jnp.int32, (16 * SPILL, 128), 0)
     lane = lax.broadcasted_iota(jnp.int32, (16 * SPILL, 128), 1)
     spilled = jnp.zeros((16 * SPILL, S), f32)
+    step_row = spill_row(lax.broadcasted_iota(jnp.int32, (16 * SPILL, 32), 0))
+    step_lane = lax.broadcasted_iota(jnp.int32, (16 * SPILL, 32), 1)
+    forward = jnp.where(step_lane == step_row, 1.0, 0.0).astype(bf16)
+    backward = jnp.where(step_lane == 31 - step_row, 1.0, 0.0).astype(bf16)
     for v in range(2):
-        taps = tap_matrix(
-            kern,
-            2 * v + 1,
-            (16 * SPILL, 128),
-            lambda row, lane: jnp.where(
-                lane >= 64, lane - spill_row(row) - 108, lane + spill_row(row) + 21
-            ),
-        )
+        wide = jnp.concatenate([tap_lines[v][1:2], jnp.zeros((1, 256), f32)], axis=1)
+        below = sheared(pltpu.roll(wide, 64, 1), 32)[:, 0:128].astype(bf16)
+        above = sheared(pltpu.roll(wide, 416, 1), 32)[:, 0:128].astype(bf16)
+        taps = jnp.where(lane >= 64, dot(forward, below), dot(backward, above))
         for s in range(4 * v, 4 * v + 4):
-            keep = (row % 16 // 2 == s) & (lane // 64 == 1 - trow[s])
+            keep = (row % 16 // 2 == s) & (lane // 64 == 1 - tile[0, v, s - 4 * v] // 2)
             spilled += dot(jnp.where(keep, taps, 0.0).astype(bf16), edges[s])
     fbuf[...] = spilled.astype(bf16)
 
@@ -197,18 +224,37 @@
         piece = s % 4
         values = pix[s].astype(f32)
         square = (values * values).astype(bf16)
-        lhs = oy[piece // 2] * wts[s, 7:8].astype(bf16)
-        rmom[piece % 2] += dot(lhs, square) * (wts[s, 15:16] * gain[s])
+        v = s // 4
+        lhs = oy[piece // 2] * row_masks[0, v, pl.ds(piece, 1), :].astype(f32).astype(bf16)
+        col_mask = col_masks[0, v, pl.ds(piece, 1), :].astype(f32)
+        rmom[piece % 2] += dot(lhs, square) * (col_mask * params[0, v, piece, 5])
         return carry
 
     lax.fori_loop(0, NS, moments, 0)
-    covers = cov[...].astype(bf16)
-    slots = dot(pp[0], covers[:, 0:256])
-    for b in range(1, 4):
-        slots += dot(pp[b], covers[:, 256 * b : 256 * b + 256])
+    row = lax.broadcasted_iota(jnp.int32, (8 * NP, 256), 0)
+    slots = jnp.zeros((8 * NP, 256), f32)
+    line = lax.broadcasted_iota(jnp.int32, (8 * NP, 128), 0)
+    codes = jnp.zeros((8 * NP, 128), f32)
+    slot_tile = jnp.zeros((8 * NP, 128), f32)
+    routes = [route[0, s // 4, s % 4] for s in range(NS)]
+    for s in range(NS):
+        rank = jnp.int32(0)
+        for before in range(s):
+            rank += (routes[before] == routes[s]).astype(jnp.int32)
+        cover = cov[s : s + 1].astype(bf16).astype(f32)
+        values = cover[:, 0:256]
+        for b in range(1, 4):
+            values = jnp.where(row % 4 == b, cover[:, 256 * b : 256 * b + 256], values)
+        slots += jnp.where((row // 8 == routes[s]) & (row % 8 // 4 == rank), values, 0.0)
+        mine = tile[0, s // 4, s % 4]
+        codes = jnp.where(line % 8 == s, (4 * routes[s] + mine).astype(f32), codes)
+        slot_tile = jnp.where(
+            (line // 8 == routes[s]) & (line % 8 // 4 == rank), mine.astype(f32), slot_tile
+        )
     small[:, 0:256] = slots
-    small[:, 256:384] = extra[...]
-    msend[...] = dot_nt(rmom[0], ox[0], precise) + dot_nt(rmom[1], ox[1], precise)
+    lane = lax.broadcasted_iota(jnp.int32, (8 * NP, 128), 1)
+    small[:, 256:384] = jnp.where(lane == 0, codes, slot_tile)
+    hess[...] = dot_nt(rmom[0], ox[0], precise) + dot_nt(rmom[1], ox[1], precise)
 
     def send_small(j, carry):
         k = lax.rem(me + j, NP)
@@ -227,32 +273,12 @@
         small.at[pl.ds(pl.multiple_of(me * 8, 8), 8)], rsmall.at[me], srecv
     ).start()
 
-    def send_moment(j, carry):
-        pltpu.make_async_remote_copy(
-            src_ref=msend,
-            dst_ref=mrecv.at[me_v],
-            send_sem=msend_sem,
-            recv_sem=mrecv_sem,
-            device_id={"visit": lax.rem(me_v + j, NV)},
-            device_id_type=MESH,
-        ).start()
-        return carry
-
-    lax.fori_loop(1, NV, send_moment, 0)
-    pltpu.make_async_copy(msend, mrecv.at[me_v], mrecv_sem).start()
-
     for v in range(2):
-        for c in range(4):
-            vmat[v, 128 * c : 128 * c + 128, :] = tap_matrix(
-                kern, 2 * v, (128, 256), lambda row, lane: row - lane + (128 * c - 108)
-            ).astype(bf16)
-
-    pltpu.make_async_copy(mrecv, mrecv, mrecv_sem).wait()
-    total = mrecv[0]
-    for v in range(1, NV):
-        total += mrecv[v]
-    hess[...] = total
-    pltpu.make_async_copy(mrecv.at[1:NV], mrecv.at[1:NV], msend_sem).wait()
+        wide = jnp.concatenate([tap_lines[v][0:1], jnp.zeros((1, 256), f32)], axis=1)
+        for c in range(2):
+            part = sheared(pltpu.roll(wide, 64 + 128 * c, 1), 128)
+            vmat[v, :, 128 * c : 128 * c + 128] = jnp.transpose(part).astype(bf16)
+
     pltpu.make_async_copy(rsmall, rsmall, srecv).wait()
     pltpu.make_async_copy(rsmall.at[1:NP], rsmall.at[1:NP], ssend).wait()
 
@@ -310,14 +336,14 @@
             part += dot(block[0 : count * rows, 128:256], vmat[v, 0:128])
             part += dot(block[2 * rows : (count + 2) * rows, 0:128], vmat[v, 384:512])
             total = part if total is None else total + part
-        return total.astype(bf16)
+        return total
 
     for t in range(2):
         for c in range(4):
             total = smooth(
                 lambda v: acc[v, t, 16 * c : 16 * c + 18].reshape(18 * ROWS, 256).astype(bf16), 16
             )
-            out[t, 16 * c : 16 * c + 16] = total.reshape(16, ROWS, 256)
+            out[t, 16 * c : 16 * c + 16] = total.astype(bf16).reshape(16, ROWS, 256)
 
     @pl.when(me < SPILL)
     def _():
@@ -342,14 +368,17 @@
             return carry
 
         lax.fori_loop(0, NP, add_spill, 0)
-        outf[...] = smooth(lambda v: accf[v].reshape(66 * 8, 256).astype(bf16), 64)
+        blocks = smooth(lambda v: accf[v].reshape(66 * 8, 256).astype(bf16), 64)
+        blocks = blocks.reshape(8, 2, 32, 256)
+        packed = blocks[:, 0] + pltpu.roll(blocks[:, 1], 4, 1)
+        outf[...] = packed.reshape(256, 256).astype(bf16)
 
 
 def owner_kernel(
-    slab, spill, wmsg, flux, weight,
+    slab, spill, wmsg, moment, pick_row, pick_col, flux, weight, hess,
     part, summed, frecv, wrecv, spart, ssum, srecv,
     part_send, part_recv, sum_send, sum_recv, wsend_sem, wrecv_sem,
-    spart_send, spart_recv, ssum_send, ssum_recv,
+    spart_send, spart_recv, ssum_send, ssum_recv, mrecv, msend_sem, mrecv_sem,
 ):
     me_v = lax.axis_index("visit")
     me = lax.axis_index("patch")
@@ -360,6 +389,66 @@
         return lax.rem(v + me // 2, NV)
 
     mine_group = group(me_v)
+    barrier = pltpu.get_barrier_semaphore()
+
+    def greet(v, p):
+        pl.semaphore_signal(
+            barrier, inc=1, device_id={"visit": v, "patch": p}, device_id_type=MESH
+        )
+
+    def greet_visit(j, carry):
+        greet(lax.rem(me_v + j, NV), me)
+        return carry
+
+    lax.fori_loop(1, NV, greet_visit, 0)
+    upper = me_v // 4
+
+    def sender(k):
+        return lax.rem(me // 2 - k // 2 + NV, NV)
+
+    for slot in range(4):
+        block = 4 * lax.rem(me_v, 4) + slot
+        k = block + upper * (NP - 1 - 2 * block)
+        v = sender(k)
+
+        @pl.when(jnp.logical_not((v == me_v) & (k == me)))
+        def _():
+            greet(v, k)
+
+    @pl.when((me_v == 3) | (me_v == 4))
+    def _():
+        def greet_spill(k, carry):
+            v = sender(k)
+
+            @pl.when(jnp.logical_not((v == me_v) & (k == me)))
+            def _():
+                greet(v, k)
+
+            return carry
+
+        lax.fori_loop(0, SPILL, greet_spill, 0)
+
+    inside = (me // 2 == mine_group).astype(jnp.int32)
+    lower_here = (me_v == me // 4).astype(jnp.int32)
+    upper_here = (me_v == 4 + (NP - 1 - me) // 4).astype(jnp.int32)
+    edge = ((me_v == 3) | (me_v == 4)).astype(jnp.int32)
+    spills = (me < SPILL).astype(jnp.int32)
+    pl.semaphore_wait(
+        barrier,
+        NV - 1 + 4 - inside * (lower_here + upper_here) + spills * (4 - inside * edge),
+    )
+
+    def send_moment(j, carry):
+        pltpu.make_async_remote_copy(
+            src_ref=moment,
+            dst_ref=mrecv.at[me_v],
+            send_sem=msend_sem,
+            recv_sem=mrecv_sem,
+            device_id={"visit": lax.rem(me_v + j, NV)},
+            device_id_type=MESH,
+        ).start()
+        return carry
+
 
     for t in range(2):
 
@@ -385,7 +474,7 @@
         def send_spill(j, carry):
             r = lax.rem(me_v + j, NV)
             pltpu.make_async_remote_copy(
-                src_ref=spill.at[pl.ds(pl.multiple_of(64 * group(r), 64), 64)],
+                src_ref=spill.at[pl.ds(pl.multiple_of(32 * group(r), 32), 32)],
                 dst_ref=spart.at[me_v],
                 send_sem=spart_send,
                 recv_sem=spart_recv,
@@ -396,7 +485,7 @@
 
         lax.fori_loop(1, NV, send_spill, 0)
         pltpu.make_async_copy(
-            spill.at[pl.ds(pl.multiple_of(64 * mine_group, 64), 64)], spart.at[me_v], spart_recv
+            spill.at[pl.ds(pl.multiple_of(32 * mine_group, 32), 32)], spart.at[me_v], spart_recv
         ).start()
 
     def send_weight(j, carry):
@@ -412,6 +501,8 @@
         return carry
 
     lax.fori_loop(1, NV, send_weight, 0)
+    lax.fori_loop(1, NV, send_moment, 0)
+    pltpu.make_async_copy(moment, mrecv.at[me_v], mrecv_sem).start()
     pltpu.make_async_copy(wmsg.at[me_v], wrecv.at[me_v], wrecv_sem).start()
 
     for t in range(2):
@@ -459,10 +550,10 @@
         total = spart[0].astype(f32)
         for v in range(1, NV):
             total += spart[v].astype(f32)
-        ssum[...] = total
+        ssum[...] = total.astype(bf16)
 
         def leg(half, t, mine):
-            src = ssum.at[32 * half : 32 * half + 32]
+            src = ssum
 
             @pl.when(jnp.logical_not(mine))
             def _():
@@ -487,6 +578,18 @@
     right = wrecv[:, :, 640:768].reshape(NV * 2 * NP, 128)
     weight[:, 0:512] = dot_tn(left, cols)
     weight[:, 512:1024] = dot_tn(right, cols)
+    pltpu.make_async_copy(mrecv, mrecv, mrecv_sem).wait()
+    total = mrecv[0]
+    for v in range(1, NV):
+        total += mrecv[v]
+    picked = dot(pick_row[...], total, precise) * pick_col[...]
+    sums = jnp.sum(picked, axis=1, keepdims=True)
+    lane = lax.broadcasted_iota(jnp.int32, (16, 128), 1)
+    matrix = jnp.zeros((16, 128), f32)
+    for q in range(10):
+        matrix = jnp.where(lane == q, sums[16 * q : 16 * q + 16], matrix)
+    hess[0] = matrix[0:10, 0:10] * (1.0 / (NV * 2 * 4 * S * S))
+    pltpu.make_async_copy(mrecv.at[1:NV], mrecv.at[1:NV], msend_sem).wait()
     pltpu.make_async_copy(frecv, frecv, sum_recv).wait()
     for slot in range(4):
         for q in range(4):
@@ -496,13 +599,19 @@
         @pl.when(me_v == 3 + t)
         def _():
             pltpu.make_async_copy(srecv, srecv, ssum_recv).wait()
+            odd = lax.rem(me, 2) == 1
             for k in range(SPILL):
+                got = srecv[k].astype(f32)
+                rows8 = [
+                    jnp.where(odd, got[8 * q + 4 : 8 * q + 8], got[8 * q : 8 * q + 4])
+                    for q in range(4)
+                ]
                 for e in range(2):
                     at = 2 * k + e
                     line = at if t == 1 else 127 - at
                     for q in range(4):
-                        flux[line : line + 1, 256 * q : 256 * q + 256] += srecv[
-                            k, 8 * q + 2 * t + e : 8 * q + 2 * t + e + 1, :
+                        flux[line : line + 1, 256 * q : 256 * q + 256] += rows8[q][
+                            2 * t + e : 2 * t + e + 1
                         ]
 
     @pl.when(me < SPILL)
@@ -512,7 +621,7 @@
         def leg_sent(half, t, mine):
             @pl.when(jnp.logical_not(mine))
             def _():
-                src = ssum.at[32 * half : 32 * half + 32]
+                src = ssum
                 pltpu.make_async_copy(src, src, ssum_send.at[t, half]).wait()
 
         spill_legs(leg_sent)
@@ -535,42 +644,18 @@
     pixels, row_mask, col_mask, route, tile, wcs_offset, subpixel, plate_scale, stretch_weight, psf_taps
 ):
     pix = pixels.reshape(NS, S, S)
-    route = route.reshape(NS)
-    tile = tile.reshape(NS)
-    gain = stretch_weight.reshape(NS).astype(f32)
-    scale = plate_scale.reshape(NS, 1, 1).astype(f32)
-    shift = wcs_offset.reshape(NS, 2, 1).astype(f32) + subpixel.reshape(NS, 2, 1).astype(f32)
-    grid_pos = jnp.arange(S).astype(f32)
-    middle = S / 2.0
-    source = scale * (grid_pos - middle) + (middle + shift)
-    lowest = jnp.floor(source) - 2.0
-    taps = jnp.arange(6).astype(f32)[None, None, :, None]
-    factor = jnp.stack([jnp.ones_like(gain), gain], axis=1)[:, :, None, None]
-    spots = lowest[:, :, None, :] + taps
-    weights = (factor * lanczos(spots - source[:, :, None, :])).astype(bf16).astype(f32)
-    masks = jnp.stack([row_mask.reshape(NS, S), col_mask.reshape(NS, S)], axis=1).astype(f32)
-    wts = jnp.concatenate([weights, lowest[:, :, None], masks[:, :, None]], axis=2)
-    wts = wts.reshape(NS, 16, S)
-    kern = (psf_taps / jnp.sum(psf_taps, axis=2, keepdims=True)).astype(bf16).astype(f32)
-    ylines = jnp.pad(kern[:, 1], ((0, 0), (44, 256 - 44 - TAPS)))
-    kern = kern.reshape(4, TAPS)
-
-    order = jnp.arange(NS)
-    rank = jnp.sum(
-        (route[:, None] == route[None, :]) & (order[None, :] < order[:, None]), axis=1
+    params = jnp.concatenate(
+        [
+            plate_scale[..., None].astype(f32),
+            wcs_offset.astype(f32),
+            subpixel.astype(f32),
+            stretch_weight[..., None].astype(f32),
+        ],
+        axis=-1,
     )
-    line = jnp.arange(8 * NP)
-    here = (route[None, :] == line[:, None] // 8) & (rank[None, :] == line[:, None] % 8 // 4)
-    pp = (
-        here[None] & ((line % 4)[None, :, None] == jnp.arange(4)[:, None, None])
-    ).astype(bf16)
-    slot_tile = jnp.sum(here * tile[None, :], axis=1).astype(f32)
-    code = (route * 4 + tile).astype(f32)
-    code_line = jnp.broadcast_to(code[None, :], (NP, 8)).reshape(8 * NP)
-    extra = jnp.where(jnp.arange(128)[None, :] == 0, code_line[:, None], slot_tile[:, None])
-
+    psf = jnp.pad(psf_taps, ((0, 0), (0, 0), (44, 256 - 44 - TAPS)))
     outer = outer_tables()
-    outer_x = jnp.pad(outer.astype(f32), ((0, 0), (0, 112), (0, 0)))
+    outer_x = np.pad(outer.astype(np.float32), ((0, 0), (0, 112), (0, 0)))
     vm = pl.BlockSpec(memory_space=pltpu.VMEM)
     sm = pl.BlockSpec(memory_space=pltpu.SMEM)
     hbm = pl.BlockSpec(memory_space=pl.ANY)
@@ -584,7 +669,7 @@
             jax.ShapeDtypeStruct((16, 128), f32),
             jax.ShapeDtypeStruct((2, 512, 256), bf16),
         ),
-        in_specs=[sm, sm, sm, vm, vm, vm, vm, vm, vm, vm],
+        in_specs=[sm, sm, sm, vm, vm, vm, vm, vm, vm],
         out_specs=(hbm, hbm, hbm, vm, vm),
         scratch_shapes=[
             pltpu.VMEM((NS, S, S), bf16),
@@ -597,23 +682,21 @@
             pltpu.VMEM((8, 2 * S), f32),
             pltpu.VMEM((2, 16, S), f32),
             pltpu.VMEM((128, 384), f32),
-            pltpu.VMEM((16, 128), f32),
-            pltpu.VMEM((NV, 16, 128), f32),
             dma((NS,)), dma((NS,)),
-            dma, dma, dma, dma, dma, dma,
+            dma, dma, dma, dma,
         ],
         compiler_params=pltpu.CompilerParams(
-            has_side_effects=True, vmem_limit_bytes=48 * 1024 * 1024
+            has_side_effects=True, vmem_limit_bytes=60 * 1024 * 1024, collective_id=1
         ),
         name="warp_send",
-    )(kern, tile // 2, gain, pix, wts, ylines, outer, outer_x, pp, extra)
+    )(params, route, tile, pix, row_mask, col_mask, psf, outer, outer_x)
 
     codes = rsmall[:, :, 256].reshape(NP * NS).astype(jnp.int32)
     slab, spill = pl.pallas_call(
         layer_kernel,
         out_shape=(
             jax.ShapeDtypeStruct((2, 64, ROWS, 256), bf16),
-            jax.ShapeDtypeStruct((512, 256), bf16),
+            jax.ShapeDtypeStruct((256, 256), bf16),
         ),
         in_specs=[sm, vm, hbm, vm],
         out_specs=(vm, vm),
@@ -637,42 +720,40 @@
     col_part = jnp.broadcast_to(covers[None, :, S:], (NV, 2 * NP, S))
     wmsg = jnp.concatenate([col_part, row_part], axis=2).astype(bf16)
 
-    flux, weight = pl.pallas_call(
+    pick_row = np.zeros((160, 16), np.float32)
+    pick_col = np.zeros((160, 128), np.float32)
+    for q in range(10):
+        for r in range(10):
+            pick_row[16 * q + r, 4 * PAIRS[q][0] + PAIRS[r][0]] = 1
+            pick_col[16 * q + r, 4 * PAIRS[q][1] + PAIRS[r][1]] = 1
+    flux, weight, hessian = pl.pallas_call(
         owner_kernel,
         out_shape=(
             jax.ShapeDtypeStruct((128, 2 * S), f32),
             jax.ShapeDtypeStruct((128, 2 * S), f32),
+            jax.ShapeDtypeStruct((1, 10, 10), f32),
         ),
-        in_specs=[vm, vm, vm],
-        out_specs=(vm, vm),
+        in_specs=[vm, vm, vm, vm, vm, vm],
+        out_specs=(vm, vm, vm),
         scratch_shapes=[
             pltpu.VMEM((2, NV, 8, ROWS, 256), bf16),
             pltpu.VMEM((2, 8, ROWS, 256), bf16),
             pltpu.VMEM((4, 4, ROWS, 256), bf16),
             pltpu.VMEM((NV, 2 * NP, 768), bf16),
-            pltpu.VMEM((NV, 64, 256), bf16),
-            pltpu.VMEM((64, 256), f32),
-            pltpu.VMEM((SPILL, 32, 256), f32),
+            pltpu.VMEM((NV, 32, 256), bf16),
+            pltpu.VMEM((32, 256), bf16),
+            pltpu.VMEM((SPILL, 32, 256), bf16),
             dma((2,)), dma((2,)), dma((2, 2)), dma, dma, dma,
             dma, dma, dma((2, 2)), dma,
+            pltpu.VMEM((NV, 16, 128), f32),
+            dma, dma,
         ],
         compiler_params=pltpu.CompilerParams(
-            has_side_effects=True, vmem_limit_bytes=48 * 1024 * 1024
+            has_side_effects=True, vmem_limit_bytes=48 * 1024 * 1024, collective_id=2
         ),
         name="owner_sum",
-    )(slab, spill, wmsg)
-
-    norm_factor = 1.0 / (NV * 2 * 4 * S * S)
-    first = np.array([pair[0] for pair in PAIRS])
-    second = np.array([pair[1] for pair in PAIRS])
-    pick_row = np.zeros((100, 16), np.float32)
-    pick_col = np.zeros((100, 16), np.float32)
-    for q in range(10):
-        for r in range(10):
-            pick_row[10 * q + r, 4 * first[q] + first[r]] = 1
-            pick_col[10 * q + r, 4 * second[q] + second[r]] = 1
-    picked = jnp.dot(pick_row, moments[:, :16], precision=precise)
-    hessian = jnp.sum(picked * pick_col, axis=1).reshape(1, 10, 10) * norm_factor
+    )(slab, spill, wmsg, moments, pick_row, pick_col)
+
     return flux, weight, hessian
 
 

time: 151 us -> 139 us (0.921); the launches traced: 149 us -> 138 us
  Pallas kernels: 132 us -> 124 us
    pallas_call x1, Pallas kernels: 69.2 us -> 61.6 us  [body(): pl.pallas_call(warp_kernel, out_shape=(jax.ShapeDtypeStruct((NP, NS, ROWS...]
    convert_element_type x4 -> x2, local copies, waits for them, and re-layouts: 2.23 us -> 0.2 us  [the longest x1 0.1 us: body(): stretch_weight[..., None].astype(f32)]
    unnamed x8 -> x14, local copies, waits for them, and re-layouts: 3.52 us -> 5.14 us
    another operation x5 -> x0, local copies, waits for them, and re-layouts: 1.59 us -> none  [the longest x2 1.5 us: body(): jnp.stack([row_mask.reshape(NS, S), col_mask.reshape(NS, S)], axis=1)]
where the time goes in v3:
time: 139 us; the launch traced here: 138 us
  Pallas kernels  124 us (89%)
  local copies, waits for them, and re-layouts  9.51 us (7%)
  other arithmetic  4.2 us (3%)
    pallas_call x1, Pallas kernels, body(): pl.pallas_call(warp_kernel, out_shape=(jax.ShapeDtypeStruct((NP, NS, ROWS...  61.6 us
    pallas_call x1, Pallas kernels, body(): pl.pallas_call(owner_kernel, out_shape=(jax.ShapeDtypeStruct((128, 2 * S)...  52 us
    pallas_call x1, Pallas kernels, body(): pl.pallas_call(layer_kernel, out_shape=(jax.ShapeDtypeStruct((2, 64, ROWS...  10.3 us
    unnamed x14, local copies, waits for them, and re-layouts  5.14 us

profile of v3, /device:TPU:29, one launch (start us, length us, event | category | flops | bytes accessed | tf_op | source)
XLA Modules:
  0.0 138.4 jit_solution(14377666803666037850)
XLA Ops:
  0.6 0.7 bitcast_convert_fusion
  1.3 0.1 copy.26
  1.4 0.8 copy.24
  2.2 0.8 copy.23
  3.0 0.7 bitcast_convert_fusion.1
  3.6 0.1 copy.25
  3.7 0.7 pad_maximum_fusion.2.params
  4.4 1.3 pad.4.psf
  5.7 61.6 %warp_send.1 = (bf16[16,8,32,512]{3,2,1,0:T(8,128)(2,1)}, bf16[16,16,512]{2,1,0:T(8,128)(2,1)}, f32[16,8,384]{2,1,0:T(8,128)}, f32[16,128]{1,0:T(8,128)}, bf16[2,512,256]{2,1,0:T(8,128)(2,1)}) custom-call(f32[1,2,4,6]{3,2,1,0:T(4,128)} %pad_maximum_fusion.2.params, s32[1,2,4]{2,1,0:T(2,128)} %route.1, s32[1,2,4]{2,1,0:T(2,128)} %tile.1, ...), custom_call_target="tpu_custom_call" | custom-call | tf_op jit(solution)/shard_map/warp_send/pallas_call | solution.py:663
  67.4 1.2 convert_reduce_fusion
  68.6 0.1 convert_element_type.63.codes
  68.7 1.0 copy-done
  69.7 0.9 copy-done.1
  70.7 10.3 %layer_smooth.1 = (bf16[2,64,32,256]{3,2,1,0:T(8,128)(2,1)S(1)}, bf16[256,256]{1,0:T(8,128)(2,1)S(1)}) custom-call(s32[128]{0:T(128)S(1)} %convert_element_type.63.codes, bf16[16,8,32,512]{3,2,1,0:T(8,128)(2,1)} %get-tuple-element.11.recv, bf16[16,16,512]{2,1,0:T(8,128)(2,1)S(1)} %copy-done.1, bf16[2,512,256]{2,1,0:T(8,128)(2,1)S(1)} %copy-done), custom_call_target="tpu_custom_call" | custom-call | tf_op jit(solution)/shard_map/layer_smooth/pallas_call | solution.py:695
  81.0 0.9 slice.18
  81.9 0.3 convert_reduce_fusion.1
  82.3 0.1 convert_element_type.65
  82.6 0.1 broadcast_and_fusion
  82.7 0.9 slice.16
  83.7 0.3 select_convert_fusion
  84.2 52.0 %owner_sum.1 = (f32[128,1024]{1,0:T(8,128)S(1)}, f32[128,1024]{1,0:T(8,128)S(1)}, f32[1,10,10]{2,1,0:T(8,128)S(1)}) custom-call(bf16[2,64,32,256]{3,2,1,0:T(8,128)(2,1)S(1)} %get-tuple-element.14.slab, bf16[256,256]{1,0:T(8,128)(2,1)S(1)} %get-tuple-element.15.spill, bf16[8,32,768]{2,1,0:T(8,128)(2,1)S(1)} %pad_maximum_fusion.wmsg, f32[16,128]{1,0:T(8,128)S(1)} %copy-done.4, ...), custom_call_target="tpu_custom_call" | custom-call | tf_op jit(solution)/shard_map/owner_sum/pallas_call | solution.py:729
  136.2 0.6 copy.28
  136.8 0.8 copy.34
  137.6 0.8 copy.35
  (21 shorter events, 0.4 us)
Async XLA Ops:
  5.7 78.4 %copy-start.3 = (f32[160,128]{1,0:T(8,128)S(1)}, f32[160,128]{1,0:T(8,128)}, u32[]{:S(2)}) copy-start(f32[160,128]{1,0:T(8,128)} %constant.55.clone.pick_col) | copy-start | bytes 245764
  67.4 16.8 %copy-start.2 = (f32[160,16]{1,0:T(8,128)S(1)}, f32[160,16]{1,0:T(8,128)}, u32[]{:S(2)}) copy-start(f32[160,16]{1,0:T(8,128)} %constant.54.clone.pick_row) | copy-start | bytes 30724
  67.4 16.8 %copy-start.4 = (f32[16,128]{1,0:T(8,128)S(1)}, f32[16,128]{1,0:T(8,128)}, u32[]{:S(2)}) copy-start(f32[16,128]{1,0:T(8,128)} %get-tuple-element.16.moment) | copy-start | bytes 24580
  68.7 1.0 copy-start
  69.7 0.9 copy-start.1

commit v4 on v3

--- a/solution.py
+++ b/solution.py
@@ -81,10 +81,10 @@
 
 
 def warp_kernel(
-    params, route, tile, pix, row_masks, col_masks, psf, oy, ox,
+    params, route, tile, pixels, row_masks, col_masks, psf, oy, ox,
     recv, rfr, rsmall, hess, vmat,
-    sbuf, fbuf, wpad, ybuf, half, edges, umat, cov, rmom, small,
-    send_sem, recv_sem, fsend, frecv, ssend, srecv,
+    pix, lines, sbuf, fbuf, wpad, ybuf, half, edges, umat, cov, rmom, small,
+    pix_sem, send_sem, recv_sem, fsend, frecv, ssend, srecv,
 ):
     me_v = lax.axis_index("visit")
     me = lax.axis_index("patch")
@@ -97,16 +97,23 @@
         return carry
 
     lax.fori_loop(1, NP, greet, 0)
-    pl.semaphore_wait(barrier, NP - 1)
+
+    def pixel_copy(s):
+        return pltpu.make_async_copy(pixels.at[s], pix.at[s], pix_sem.at[s])
+
+    for s in range(NS):
+        pixel_copy(s).start()
+    lines[...] = jnp.zeros_like(lines)
     wpad[0:192, :] = jnp.zeros((192, S), bf16)
     wpad[704:896, :] = jnp.zeros((192, S), bf16)
     rmom[...] = jnp.zeros_like(rmom)
     tap_lines = []
     for v in range(2):
-        lines = psf[v] / jnp.sum(psf[v], axis=1, keepdims=True)
-        lines = lines.astype(bf16).astype(f32)
-        tap_lines.append(lines)
-        umat[v] = sheared(lines[1:2], 128).astype(bf16)
+        kernels = psf[v] / jnp.sum(psf[v], axis=1, keepdims=True)
+        lines[2 * v : 2 * v + 2, 0:TAPS] = kernels.astype(bf16).astype(f32)
+        placed = pltpu.roll(lines[...], 44, 1)
+        tap_lines.append(placed[2 * v : 2 * v + 2])
+        umat[v] = sheared(placed[2 * v + 1 : 2 * v + 2], 128).astype(bf16)
 
     def stretch(s):
         v = s // 4
@@ -123,6 +130,7 @@
             return jnp.where(tap == 6.0, lowest, value)
 
         columns = jnp.transpose(weights_along(0, 1.0))
+        pixel_copy(s).wait()
         wt = weights_along(1, params[0, v, piece, 5])
         row_mask = row_masks[0, v, pl.ds(piece, 1), :].astype(f32)
         col_mask = col_masks[0, v, pl.ds(piece, 1), :].astype(f32)
@@ -158,9 +166,7 @@
 
     turn = 7 * me + 3 * me_v
 
-    def step(s, carry):
-        stretch(s)
-
+    def send_slabs(s):
         def send(j, carry):
             k = lax.rem(me + 1 + lax.rem(turn + j, NP - 1), NP)
             pltpu.make_async_remote_copy(
@@ -177,9 +183,17 @@
         pltpu.make_async_copy(
             sbuf.at[s, pl.ds(pl.multiple_of(me * ROWS, ROWS), ROWS)], recv.at[me, s], recv_sem.at[s]
         ).start()
-        return carry
-
-    lax.fori_loop(0, NS, step, 0)
+
+    stretch(0)
+    pl.semaphore_wait(barrier, NP - 1)
+
+    def step(s, carry):
+        send_slabs(s)
+        stretch(s + 1)
+        return carry
+
+    lax.fori_loop(0, NS - 1, step, 0)
+    send_slabs(NS - 1)
 
     row = lax.broadcasted_iota(jnp.int32, (16 * SPILL, 128), 0)
     lane = lax.broadcasted_iota(jnp.int32, (16 * SPILL, 128), 1)
@@ -302,8 +316,39 @@
         pltpu.make_async_copy(fbuf, fbuf, fsend).wait()
 
 
-def layer_kernel(codes, recv, rfr, vmat, out, outf, acc, accf, fvm, sem):
+def layer_kernel(
+    codes, slabs, rfr, vmat, slots, out, outf, wmsg, recv, acc, accf, fvm, slab_sem, sem
+):
     me = lax.axis_index("patch")
+    spill_copy = pltpu.make_async_copy(rfr, fvm, sem)
+
+    @pl.when(me < SPILL)
+    def _():
+        spill_copy.start()
+
+    def slab_copy(i):
+        part = pl.ds(4 * i, 4)
+        return pltpu.make_async_copy(slabs.at[part], recv.at[part], slab_sem.at[i])
+
+    for i in range(4):
+        slab_copy(i).start()
+
+    for q in range(2):
+        rows = [slots[:, 4 * q + b, 0:256] for b in range(4)]
+        tiles = slots[:, 4 * q, 256:384][:, 1:2]
+        at = slice(NP * q, NP * q + NP)
+        cols = [rows[2].astype(bf16), rows[3].astype(bf16)]
+        for r in range(NV):
+            quarter = r % 4
+            wmsg[r, at, 0:256] = cols[0]
+            wmsg[r, at, 256:512] = cols[1]
+            piece = rows[quarter // 2][:, 128 * (quarter % 2) : 128 * (quarter % 2) + 128]
+            for side in range(2):
+                mine = tiles == float(2 * (r // 4) + side)
+                wmsg[r, at, 512 + 128 * side : 640 + 128 * side] = jnp.where(
+                    mine, piece, 0.0
+                ).astype(bf16)
+
     zero = jnp.zeros((ROWS, 256), f32)
 
     def clear(b, carry):
@@ -312,7 +357,7 @@
                 acc[v, t, b] = zero
         return carry
 
-    lax.fori_loop(0, 66, clear, 0)
+    lax.fori_loop(0, 66, clear, 0, unroll=2)
 
     def add(at, carry):
         s = at % NS
@@ -325,7 +370,9 @@
         acc[s // 4, t, 2 * g + 2] += data[:, 256:512]
         return carry
 
-    lax.fori_loop(0, NP * NS, add, 0)
+    for i in range(4):
+        slab_copy(i).wait()
+        lax.fori_loop(4 * i * NS, 4 * (i + 1) * NS, add, 0, unroll=4)
 
     def smooth(blocks_of, count):
         total = None
@@ -347,10 +394,8 @@
 
     @pl.when(me < SPILL)
     def _():
-        copy = pltpu.make_async_copy(rfr, fvm, sem)
-        copy.start()
         accf[...] = jnp.zeros_like(accf)
-        copy.wait()
+        spill_copy.wait()
         target = lax.broadcasted_iota(jnp.int32, (8, S), 0) // 2
 
         def add_spill(c, carry):
@@ -653,7 +698,6 @@
         ],
         axis=-1,
     )
-    psf = jnp.pad(psf_taps, ((0, 0), (0, 0), (44, 256 - 44 - TAPS)))
     outer = outer_tables()
     outer_x = np.pad(outer.astype(np.float32), ((0, 0), (0, 112), (0, 0)))
     vm = pl.BlockSpec(memory_space=pltpu.VMEM)
@@ -669,9 +713,11 @@
             jax.ShapeDtypeStruct((16, 128), f32),
             jax.ShapeDtypeStruct((2, 512, 256), bf16),
         ),
-        in_specs=[sm, sm, sm, vm, vm, vm, vm, vm, vm],
+        in_specs=[sm, sm, sm, hbm, vm, vm, vm, vm, vm],
         out_specs=(hbm, hbm, hbm, vm, vm),
         scratch_shapes=[
+            pltpu.VMEM((NS, S, S), bf16),
+            pltpu.VMEM((8, 256), f32),
             pltpu.VMEM((NS, S, S), bf16),
             pltpu.VMEM((16 * SPILL, S), bf16),
             pltpu.VMEM((896, S), bf16),
@@ -682,43 +728,36 @@
             pltpu.VMEM((8, 2 * S), f32),
             pltpu.VMEM((2, 16, S), f32),
             pltpu.VMEM((128, 384), f32),
-            dma((NS,)), dma((NS,)),
+            dma((NS,)), dma((NS,)), dma((NS,)),
             dma, dma, dma, dma,
         ],
         compiler_params=pltpu.CompilerParams(
             has_side_effects=True, vmem_limit_bytes=60 * 1024 * 1024, collective_id=1
         ),
         name="warp_send",
-    )(params, route, tile, pix, row_mask, col_mask, psf, outer, outer_x)
+    )(params, route, tile, pix, row_mask, col_mask, psf_taps, outer, outer_x)
 
     codes = rsmall[:, :, 256].reshape(NP * NS).astype(jnp.int32)
-    slab, spill = pl.pallas_call(
+    slab, spill, wmsg = pl.pallas_call(
         layer_kernel,
         out_shape=(
             jax.ShapeDtypeStruct((2, 64, ROWS, 256), bf16),
             jax.ShapeDtypeStruct((256, 256), bf16),
+            jax.ShapeDtypeStruct((NV, 2 * NP, 768), bf16),
         ),
-        in_specs=[sm, vm, hbm, vm],
-        out_specs=(vm, vm),
+        in_specs=[sm, hbm, hbm, vm, vm],
+        out_specs=(vm, vm, vm),
         scratch_shapes=[
+            pltpu.VMEM((NP, NS, ROWS, S), bf16),
             pltpu.VMEM((2, 2, 66, ROWS, 256), f32),
             pltpu.VMEM((2, 66, 8, 256), f32),
             pltpu.VMEM((NP, 16, S), bf16),
+            dma((4,)),
             dma,
         ],
-        compiler_params=pltpu.CompilerParams(vmem_limit_bytes=48 * 1024 * 1024),
+        compiler_params=pltpu.CompilerParams(vmem_limit_bytes=60 * 1024 * 1024),
         name="layer_smooth",
-    )(codes, recv, rfr, vmat)
-
-    covers = rsmall[:, :, 0:256].reshape(2 * NP, 2 * S)
-    tiles = rsmall[:, ::4, 257].reshape(1, 2 * NP, 1, 1).astype(jnp.int32)
-    owner = jnp.arange(NV)[:, None, None, None]
-    keep = (tiles // 2 == owner // 4) & (tiles % 2 == jnp.arange(2)[None, None, :, None])
-    row_part = covers[:, :S].reshape(2 * NP, 4, 128).transpose(1, 0, 2)
-    row_part = jnp.concatenate([row_part, row_part], axis=0)
-    row_part = jnp.where(keep, row_part[:, :, None, :], 0.0).reshape(NV, 2 * NP, 256)
-    col_part = jnp.broadcast_to(covers[None, :, S:], (NV, 2 * NP, S))
-    wmsg = jnp.concatenate([col_part, row_part], axis=2).astype(bf16)
+    )(codes, recv, rfr, vmat, rsmall)
 
     pick_row = np.zeros((160, 16), np.float32)
     pick_col = np.zeros((160, 128), np.float32)
@@ -733,7 +772,7 @@
             jax.ShapeDtypeStruct((128, 2 * S), f32),
             jax.ShapeDtypeStruct((1, 10, 10), f32),
         ),
-        in_specs=[vm, vm, vm, vm, vm, vm],
+        in_specs=[hbm, hbm, hbm, hbm, vm, vm],
         out_specs=(vm, vm, vm),
         scratch_shapes=[
             pltpu.VMEM((2, NV, 8, ROWS, 256), bf16),

time: 139 us -> 135 us (0.971)
  local copies, waits for them, and re-layouts: 9.51 us -> 8.04 us
    pallas_call x1, Pallas kernels: 61.6 us -> 58 us  [body(): pl.pallas_call(warp_kernel, out_shape=(jax.ShapeDtypeStruct((NP, NS, ROWS...]
    pallas_call x1, Pallas kernels: 52 us -> 54.2 us  [body(): pl.pallas_call(owner_kernel, out_shape=(jax.ShapeDtypeStruct((128, 2 * S)...]
    slice x3 -> x0, local copies, waits for them, and re-layouts: 1.86 us -> none  [the longest x1 0.94 us: body(): tiles = rsmall[:, ::4, 257].reshape(1, 2 * NP, 1, 1).astype(jnp.int32)]
    unnamed x14 -> x16, local copies, waits for them, and re-layouts: 5.14 us -> 6.64 us
where the time goes in v4:
time: 135 us
  Pallas kernels  123 us (91%)
  local copies, waits for them, and re-layouts  8.04 us (6%)
  other arithmetic  3.19 us (2%)
    pallas_call x1, Pallas kernels, body(): pl.pallas_call(warp_kernel, out_shape=(jax.ShapeDtypeStruct((NP, NS, ROWS...  58 us
    pallas_call x1, Pallas kernels, body(): pl.pallas_call(owner_kernel, out_shape=(jax.ShapeDtypeStruct((128, 2 * S)...  54.2 us
    pallas_call x1, Pallas kernels, body(): pl.pallas_call(layer_kernel, out_shape=(jax.ShapeDtypeStruct((2, 64, ROWS...  10.4 us
    unnamed x16, local copies, waits for them, and re-layouts  6.64 us

profile of v4, /device:TPU:29, one launch (start us, length us, event | category | flops | bytes accessed | tf_op | source)
XLA Modules:
  0.0 134.6 jit_solution(13089988641677903951)
XLA Ops:
  0.6 0.7 bitcast_convert_fusion.1
  1.3 0.7 bitcast_convert_fusion
  1.9 0.8 copy.23
  2.7 0.1 copy.25
  2.8 0.1 copy.24
  2.9 0.8 copy.22
  3.7 0.7 pad_maximum_fusion.params
  4.4 0.0 copy-start.3
  4.4 58.0 %warp_send.1 = (bf16[16,8,32,512]{3,2,1,0:T(8,128)(2,1)}, bf16[16,16,512]{2,1,0:T(8,128)(2,1)}, f32[16,8,384]{2,1,0:T(8,128)}, f32[16,128]{1,0:T(8,128)}, bf16[2,512,256]{2,1,0:T(8,128)(2,1)}) custom-call(f32[1,2,4,6]{3,2,1,0:T(4,128)} %pad_maximum_fusion.params, s32[1,2,4]{2,1,0:T(2,128)} %route.1, s32[1,2,4]{2,1,0:T(2,128)} %tile.1, ...), custom_call_target="tpu_custom_call" | custom-call | tf_op jit(solution)/shard_map/warp_send/pallas_call | solution.py:707
  62.4 0.0 copy-start.5
  62.4 1.2 convert_reduce_fusion
  63.6 0.6 convert_element_type.46.codes
  64.2 10.4 %layer_smooth.1 = (bf16[2,64,32,256]{3,2,1,0:T(8,128)(2,1)}, bf16[256,256]{1,0:T(8,128)(2,1)}, bf16[8,32,768]{2,1,0:T(8,128)(2,1)}) custom-call(s32[128]{0:T(128)} %convert_element_type.46.codes, bf16[16,8,32,512]{3,2,1,0:T(8,128)(2,1)} %get-tuple-element.12.slabs, bf16[16,16,512]{2,1,0:T(8,128)(2,1)} %get-tuple-element.13.rfr, ...), custom_call_target="tpu_custom_call" | custom-call | tf_op jit(solution)/shard_map/layer_smooth/pallas_call | solution.py:741
  74.6 0.0 copy-done.3
  74.7 0.0 copy-done.4
  74.7 0.0 copy-done.5
  74.7 0.0 copy-start
  74.7 1.6 %copy-done = bf16[2,64,32,256]{3,2,1,0:T(8,128)(2,1)S(1)} copy-done((bf16[2,64,32,256]{3,2,1,0:T(8,128)(2,1)S(1)}, bf16[2,64,32,256]{3,2,1,0:T(8,128)(2,1)}, u32[]{:S(2)}) %copy-start) | copy-done | bytes 2097176
  76.3 1.0 copy-done.1
  77.3 0.9 copy-done.2
  78.2 54.2 %owner_sum.1 = (f32[128,1024]{1,0:T(8,128)S(1)}, f32[128,1024]{1,0:T(8,128)S(1)}, f32[1,10,10]{2,1,0:T(8,128)S(1)}) custom-call(bf16[2,64,32,256]{3,2,1,0:T(8,128)(2,1)S(1)} %copy-done, bf16[256,256]{1,0:T(8,128)(2,1)S(1)} %copy-done.2, bf16[8,32,768]{2,1,0:T(8,128)(2,1)S(1)} %copy-done.1, f32[16,128]{1,0:T(8,128)S(1)} %copy-done.5, ...), custom_call_target="tpu_custom_call" | custom-call | tf_op jit(solution)/shard_map/owner_sum/pallas_call | solution.py:768
  132.4 0.6 copy.26
  133.0 0.8 copy.29
  133.8 0.8 copy.30
  (5 shorter events, 0.0 us)
Async XLA Ops:
  4.4 70.3 %copy-start.3 = (f32[160,128]{1,0:T(8,128)S(1)}, f32[160,128]{1,0:T(8,128)}, u32[]{:S(2)}) copy-start(f32[160,128]{1,0:T(8,128)} %constant.11.clone.pick_col) | copy-start | bytes 245764
  4.4 70.3 %copy-start.4 = (f32[160,16]{1,0:T(8,128)S(1)}, f32[160,16]{1,0:T(8,128)}, u32[]{:S(2)}) copy-start(f32[160,16]{1,0:T(8,128)} %constant.10.clone.pick_row) | copy-start | bytes 30724
  62.4 12.3 %copy-start.5 = (f32[16,128]{1,0:T(8,128)S(1)}, f32[16,128]{1,0:T(8,128)}, u32[]{:S(2)}) copy-start(f32[16,128]{1,0:T(8,128)} %get-tuple-element.18.moment) | copy-start | bytes 24580
  74.7 1.6 %copy-start = (bf16[2,64,32,256]{3,2,1,0:T(8,128)(2,1)S(1)}, bf16[2,64,32,256]{3,2,1,0:T(8,128)(2,1)}, u32[]{:S(2)}) copy-start(bf16[2,64,32,256]{3,2,1,0:T(8,128)(2,1)} %get-tuple-element.15.slab) | copy-start | bytes 6291460
  76.3 1.0 copy-start.1
  77.3 0.9 copy-start.2

commit v5 on v4

--- a/solution.py
+++ b/solution.py
@@ -495,25 +495,6 @@
         return carry
 
 
-    for t in range(2):
-
-        def send_part(j, carry):
-            r = lax.rem(me_v + 1 + lax.rem(turn + j, NV - 1), NV)
-            pltpu.make_async_remote_copy(
-                src_ref=slab.at[t, pl.ds(8 * group(r), 8)],
-                dst_ref=part.at[t, me_v],
-                send_sem=part_send.at[t],
-                recv_sem=part_recv.at[t],
-                device_id={"visit": r},
-                device_id_type=MESH,
-            ).start()
-            return carry
-
-        lax.fori_loop(0, NV - 1, send_part, 0)
-        pltpu.make_async_copy(
-            slab.at[t, pl.ds(8 * mine_group, 8)], part.at[t, me_v], part_recv.at[t]
-        ).start()
-
     @pl.when(me < SPILL)
     def _():
         def send_spill(j, carry):
@@ -533,6 +514,28 @@
             spill.at[pl.ds(pl.multiple_of(32 * mine_group, 32), 32)], spart.at[me_v], spart_recv
         ).start()
 
+    for t in range(2):
+        for half in range(2):
+
+            def send_part(j, carry):
+                r = lax.rem(me_v + 1 + lax.rem(turn + j, NV - 1), NV)
+                pltpu.make_async_remote_copy(
+                    src_ref=slab.at[t, pl.ds(8 * group(r) + 4 * half, 4)],
+                    dst_ref=part.at[t, half, me_v],
+                    send_sem=part_send.at[t, half],
+                    recv_sem=part_recv.at[t, half],
+                    device_id={"visit": r},
+                    device_id_type=MESH,
+                ).start()
+                return carry
+
+            lax.fori_loop(0, NV - 1, send_part, 0)
+            pltpu.make_async_copy(
+                slab.at[t, pl.ds(8 * mine_group + 4 * half, 4)],
+                part.at[t, half, me_v],
+                part_recv.at[t, half],
+            ).start()
+
     def send_weight(j, carry):
         r = lax.rem(me_v + j, NV)
         pltpu.make_async_remote_copy(
@@ -550,21 +553,56 @@
     pltpu.make_async_copy(moment, mrecv.at[me_v], mrecv_sem).start()
     pltpu.make_async_copy(wmsg.at[me_v], wrecv.at[me_v], wrecv_sem).start()
 
+    def spill_legs(act):
+        for half in range(2):
+            for t in range(2):
+                act(half, t, (me_v == 3 + t) & (me == 2 * mine_group + half))
+
+    @pl.when(me < SPILL)
+    def _():
+        pltpu.make_async_copy(spart, spart, spart_recv).wait()
+        total = spart[0].astype(f32)
+        for v in range(1, NV):
+            total += spart[v].astype(f32)
+        ssum[...] = total.astype(bf16)
+
+        def leg(half, t, mine):
+            src = ssum
+
+            @pl.when(jnp.logical_not(mine))
+            def _():
+                pltpu.make_async_remote_copy(
+                    src_ref=src,
+                    dst_ref=srecv.at[me],
+                    send_sem=ssum_send.at[t, half],
+                    recv_sem=ssum_recv,
+                    device_id={"visit": 3 + t, "patch": 2 * mine_group + half},
+                    device_id_type=MESH,
+                ).start()
+
+            @pl.when(mine)
+            def _():
+                pltpu.make_async_copy(src, srecv.at[me], ssum_recv).start()
+
+        spill_legs(leg)
+
     for t in range(2):
         block = me if t == 0 else NP - 1 - me
         r = 4 * t + block // 4
         slot = lax.rem(block, 4)
-        pltpu.make_async_copy(part.at[t], part.at[t], part_recv.at[t]).wait()
-
-        def add(b, carry):
-            total = part[t, 0, b].astype(f32)
-            for v in range(1, NV):
-                total += part[t, v, b].astype(f32)
-            summed[t, b] = total.astype(bf16)
-            return carry
-
-        lax.fori_loop(0, 8, add, 0)
         for half in range(2):
+            pltpu.make_async_copy(
+                part.at[t, half], part.at[t, half], part_recv.at[t, half]
+            ).wait()
+
+            def add(b, carry):
+                total = part[t, half, 0, b].astype(f32)
+                for v in range(1, NV):
+                    total += part[t, half, v, b].astype(f32)
+                summed[t, 4 * half + b] = total.astype(bf16)
+                return carry
+
+            lax.fori_loop(0, 4, add, 0)
             p = 2 * mine_group + half
             mine = (r == me_v) & (p == me)
             src = summed.at[t, 4 * half : 4 * half + 4]
@@ -583,39 +621,6 @@
             @pl.when(mine)
             def _():
                 pltpu.make_async_copy(src, frecv.at[slot], sum_recv).start()
-
-    def spill_legs(act):
-        for half in range(2):
-            for t in range(2):
-                act(half, t, (me_v == 3 + t) & (me == 2 * mine_group + half))
-
-    @pl.when(me < SPILL)
-    def _():
-        pltpu.make_async_copy(spart, spart, spart_recv).wait()
-        total = spart[0].astype(f32)
-        for v in range(1, NV):
-            total += spart[v].astype(f32)
-        ssum[...] = total.astype(bf16)
-
-        def leg(half, t, mine):
-            src = ssum
-
-            @pl.when(jnp.logical_not(mine))
-            def _():
-                pltpu.make_async_remote_copy(
-                    src_ref=src,
-                    dst_ref=srecv.at[me],
-                    send_sem=ssum_send.at[t, half],
-                    recv_sem=ssum_recv,
-                    device_id={"visit": 3 + t, "patch": 2 * mine_group + half},
-                    device_id_type=MESH,
-                ).start()
-
-            @pl.when(mine)
-            def _():
-                pltpu.make_async_copy(src, srecv.at[me], ssum_recv).start()
-
-        spill_legs(leg)
 
     pltpu.make_async_copy(wrecv, wrecv, wrecv_sem).wait()
     cols = wrecv[:, :, 0:512].reshape(NV * 2 * NP, 512)
@@ -675,8 +680,9 @@
     for t in range(2):
         block = me if t == 0 else NP - 1 - me
         r = 4 * t + block // 4
-        pltpu.make_async_copy(part.at[t, 1:NV], part.at[t, 1:NV], part_send.at[t]).wait()
         for half in range(2):
+            others = part.at[t, half, 1:NV]
+            pltpu.make_async_copy(others, others, part_send.at[t, half]).wait()
             mine = (r == me_v) & (2 * mine_group + half == me)
 
             @pl.when(jnp.logical_not(mine))
@@ -775,14 +781,14 @@
         in_specs=[hbm, hbm, hbm, hbm, vm, vm],
         out_specs=(vm, vm, vm),
         scratch_shapes=[
-            pltpu.VMEM((2, NV, 8, ROWS, 256), bf16),
+            pltpu.VMEM((2, 2, NV, 4, ROWS, 256), bf16),
             pltpu.VMEM((2, 8, ROWS, 256), bf16),
             pltpu.VMEM((4, 4, ROWS, 256), bf16),
             pltpu.VMEM((NV, 2 * NP, 768), bf16),
             pltpu.VMEM((NV, 32, 256), bf16),
             pltpu.VMEM((32, 256), bf16),
             pltpu.VMEM((SPILL, 32, 256), bf16),
-            dma((2,)), dma((2,)), dma((2, 2)), dma, dma, dma,
+            dma((2, 2)), dma((2, 2)), dma((2, 2)), dma, dma, dma,
             dma, dma, dma((2, 2)), dma,
             pltpu.VMEM((NV, 16, 128), f32),
             dma, dma,

time: 135 us -> 129 us (0.956)
  the two profiles are of different devices: /device:TPU:29 before, /device:TPU:6 now
where the time goes in v5:
time: 129 us
  Pallas kernels  117 us (91%)
  local copies, waits for them, and re-layouts  8.04 us (6%)
  other arithmetic  3.19 us (2%)
    pallas_call x1, Pallas kernels, body(): pl.pallas_call(warp_kernel, out_shape=(jax.ShapeDtypeStruct((NP, NS, ROWS...  59.4 us
    pallas_call x1, Pallas kernels, body(): pl.pallas_call(owner_kernel, out_shape=(jax.ShapeDtypeStruct((128, 2 * S)...  44.9 us
    pallas_call x1, Pallas kernels, body(): pl.pallas_call(layer_kernel, out_shape=(jax.ShapeDtypeStruct((2, 64, ROWS...  12.7 us
    unnamed x16, local copies, waits for them, and re-layouts  6.64 us

profile of v5, /device:TPU:6, one launch (start us, length us, event | category | flops | bytes accessed | tf_op | source)
XLA Modules:
  0.0 128.9 jit_solution(15510863089640051467)
XLA Ops:
  0.6 0.7 bitcast_convert_fusion.1
  1.3 0.7 bitcast_convert_fusion
  1.9 0.8 copy.23
  2.7 0.1 copy.25
  2.8 0.1 copy.24
  2.9 0.8 copy.22
  3.7 0.7 pad_maximum_fusion.params
  4.4 0.0 copy-start.3
  4.4 59.4 %warp_send.1 = (bf16[16,8,32,512]{3,2,1,0:T(8,128)(2,1)}, bf16[16,16,512]{2,1,0:T(8,128)(2,1)}, f32[16,8,384]{2,1,0:T(8,128)}, f32[16,128]{1,0:T(8,128)}, bf16[2,512,256]{2,1,0:T(8,128)(2,1)}) custom-call(f32[1,2,4,6]{3,2,1,0:T(4,128)} %pad_maximum_fusion.params, s32[1,2,4]{2,1,0:T(2,128)} %route.1, s32[1,2,4]{2,1,0:T(2,128)} %tile.1, ...), custom_call_target="tpu_custom_call" | custom-call | tf_op jit(solution)/shard_map/warp_send/pallas_call | solution.py:713
  63.8 0.0 copy-start.5
  63.8 1.2 convert_reduce_fusion
  65.0 0.6 convert_element_type.46.codes
  65.6 12.7 %layer_smooth.1 = (bf16[2,64,32,256]{3,2,1,0:T(8,128)(2,1)}, bf16[256,256]{1,0:T(8,128)(2,1)}, bf16[8,32,768]{2,1,0:T(8,128)(2,1)}) custom-call(s32[128]{0:T(128)} %convert_element_type.46.codes, bf16[16,8,32,512]{3,2,1,0:T(8,128)(2,1)} %get-tuple-element.12.slabs, bf16[16,16,512]{2,1,0:T(8,128)(2,1)} %get-tuple-element.13.rfr, ...), custom_call_target="tpu_custom_call" | custom-call | tf_op jit(solution)/shard_map/layer_smooth/pallas_call | solution.py:747
  78.3 0.0 copy-done.3
  78.3 0.0 copy-done.4
  78.3 0.0 copy-done.5
  78.3 0.0 copy-start
  78.3 1.6 %copy-done = bf16[2,64,32,256]{3,2,1,0:T(8,128)(2,1)S(1)} copy-done((bf16[2,64,32,256]{3,2,1,0:T(8,128)(2,1)S(1)}, bf16[2,64,32,256]{3,2,1,0:T(8,128)(2,1)}, u32[]{:S(2)}) %copy-start) | copy-done | bytes 2097176
  79.9 1.0 copy-done.1
  80.9 0.9 copy-done.2
  81.8 44.9 %owner_sum.1 = (f32[128,1024]{1,0:T(8,128)S(1)}, f32[128,1024]{1,0:T(8,128)S(1)}, f32[1,10,10]{2,1,0:T(8,128)S(1)}) custom-call(bf16[2,64,32,256]{3,2,1,0:T(8,128)(2,1)S(1)} %copy-done, bf16[256,256]{1,0:T(8,128)(2,1)S(1)} %copy-done.2, bf16[8,32,768]{2,1,0:T(8,128)(2,1)S(1)} %copy-done.1, f32[16,128]{1,0:T(8,128)S(1)} %copy-done.5, ...), custom_call_target="tpu_custom_call" | custom-call | tf_op jit(solution)/shard_map/owner_sum/pallas_call | solution.py:774
  126.7 0.6 copy.26
  127.3 0.8 copy.29
  128.1 0.8 copy.30
  (5 shorter events, 0.0 us)
Async XLA Ops:
  4.4 73.9 %copy-start.3 = (f32[160,128]{1,0:T(8,128)S(1)}, f32[160,128]{1,0:T(8,128)}, u32[]{:S(2)}) copy-start(f32[160,128]{1,0:T(8,128)} %constant.11.clone.pick_col) | copy-start | bytes 245764
  4.4 73.9 %copy-start.4 = (f32[160,16]{1,0:T(8,128)S(1)}, f32[160,16]{1,0:T(8,128)}, u32[]{:S(2)}) copy-start(f32[160,16]{1,0:T(8,128)} %constant.10.clone.pick_row) | copy-start | bytes 30724
  63.8 14.5 %copy-start.5 = (f32[16,128]{1,0:T(8,128)S(1)}, f32[16,128]{1,0:T(8,128)}, u32[]{:S(2)}) copy-start(f32[16,128]{1,0:T(8,128)} %get-tuple-element.18.moment) | copy-start | bytes 24580
  78.3 1.6 %copy-start = (bf16[2,64,32,256]{3,2,1,0:T(8,128)(2,1)S(1)}, bf16[2,64,32,256]{3,2,1,0:T(8,128)(2,1)}, u32[]{:S(2)}) copy-start(bf16[2,64,32,256]{3,2,1,0:T(8,128)(2,1)} %get-tuple-element.15.slab) | copy-start | bytes 6291460
  79.9 1.0 copy-start.1
  80.9 0.9 copy-start.2
